TPU v7x, 32 devices: a whole 2x2x4 slice. The times are simulated.
32 devices in a mesh: cfg: 2 (over y), space: 8 (over z, x), tm: 2 (over core).
Axes of the slice: x: 2, y: 2, z: 4, core: 2. Of those that a mesh axis runs over, the one named last changes fastest.
Arguments:
- solutions: float32 [4, 4, 2, 3, 8, 2048], P(('cfg', 'tm'), None, None, None, 'space'), parts along dimension 0, may hold values from -16 to 16
- links: float32 [4, 3, 2, 3, 3, 8, 2048], P(('cfg', 'tm'), None, None, None, None, 'space'), parts along dimension 0, may hold values from -0.75 to 1.75
- eigvecs: bfloat16 [4, 128, 2, 3, 8, 2048], P(('cfg', 'tm'), 'space'), parts along dimension 0, may hold values from -0.01953125 to 0.01953125
Outputs:
- smeared: bfloat16 [4, 4, 2, 3, 8, 2048], P(('cfg', 'tm'), None, None, None, 'space'), parts along dimension 0
- coefficients: float32 [4, 128, 8], P(('cfg', 'tm'), 'space'), parts along dimension 0
There are 2 independent parts, one for each index of `cfg`. A program takes and returns all parts, laid end to end along the dimension named above; each array names one. Nothing has to cross between parts.
All inputs are finite; a program needn't handle non-finite values.
Results may differ from a plain program's by a relative error of at most 0.0045.
Values may be sent and summed in bfloat16 or wider, within the bound.
No kernel may reach another device: no remote copies, remote signals or barrier semaphores. Data moves between devices by JAX's collectives and lax.ppermute only.
A program may use at most 192 MiB of HBM per device.

v0:
```python
import jax
import jax.numpy as jnp
from jax import lax
from jax.sharding import PartitionSpec as P

NSMEAR = 4
LX = 64


kappa_hop = 0.1


def swapped_2(block, axis, stride):
    count = lax.axis_size(axis)
    route = []
    for low in range(count):
        high = low | 1 << stride
        if high != low and high < count:
            route += [(low, high), (high, low)]
    return lax.ppermute(block, axis, route)


def for_sending(array):

    def short(part):
        return part.astype(jnp.bfloat16) if part.dtype == jnp.float32 else part

    return jax.tree.map(short, array)


def from_behind(block, axis, distance):
    devices = range(lax.axis_size(axis))
    route = [((i - distance) % len(devices), i) for i in devices]
    return lax.ppermute(block, axis, route)


def color_product(link_real, link_imag, field_real, field_imag):
    out_real = None
    out_imag = None
    for inner in range(3):
        column_real = link_real[:, None, :, inner]
        column_imag = link_imag[:, None, :, inner]
        entry_real = field_real[:, :, inner : inner + 1]
        entry_imag = field_imag[:, :, inner : inner + 1]
        term_real = column_real * entry_real - column_imag * entry_imag
        term_imag = column_real * entry_imag + column_imag * entry_real
        if out_real is None:
            out_real = term_real
            out_imag = term_imag
        else:
            out_real = out_real + term_real
            out_imag = out_imag + term_imag
    return (out_real, out_imag)


def adjoint_product(link_real, link_imag, field_real, field_imag):
    return color_product(
        jnp.swapaxes(link_real, 1, 2), -jnp.swapaxes(link_imag, 1, 2), field_real, field_imag
    )


def hopping(real, imag, link_flat):
    sites = real.shape[-1]
    x_place = lax.broadcasted_iota(jnp.int32, (sites,), 0) % LX
    at_end = x_place == LX - 1
    at_start = x_place == 0
    link_real = link_flat[:, 0, 0]
    link_imag = link_flat[:, 0, 1]
    next_real = jnp.where(at_end, jnp.roll(real, LX - 1, 3), jnp.roll(real, -1, 3))
    next_imag = jnp.where(at_end, jnp.roll(imag, LX - 1, 3), jnp.roll(imag, -1, 3))
    ahead_real, ahead_imag = color_product(link_real, link_imag, next_real, next_imag)
    back_real, back_imag = adjoint_product(link_real, link_imag, real, imag)
    total_real = ahead_real + jnp.where(
        at_start, jnp.roll(back_real, 1 - LX, 3), jnp.roll(back_real, 1, 3)
    )
    total_imag = ahead_imag + jnp.where(
        at_start, jnp.roll(back_imag, 1 - LX, 3), jnp.roll(back_imag, 1, 3)
    )
    link_real = link_flat[:, 1, 0]
    link_imag = link_flat[:, 1, 1]
    back_real, back_imag = adjoint_product(link_real, link_imag, real, imag)
    edge_rows = jnp.stack(
        [real[..., :LX], imag[..., :LX], back_real[..., sites - LX :], back_imag[..., sites - LX :]]
    )
    edges = swapped_2(edge_rows, "space", 0)
    next_real = jnp.concatenate([real[..., LX:], edges[0]], axis=3)
    next_imag = jnp.concatenate([imag[..., LX:], edges[1]], axis=3)
    ahead_real, ahead_imag = color_product(link_real, link_imag, next_real, next_imag)
    total_real = (
        total_real + ahead_real + jnp.concatenate([edges[2], back_real[..., : sites - LX]], axis=3)
    )
    total_imag = (
        total_imag + ahead_imag + jnp.concatenate([edges[3], back_imag[..., : sites - LX]], axis=3)
    )
    link_real = link_flat[:, 2, 0]
    link_imag = link_flat[:, 2, 1]
    upper = from_behind(for_sending(jnp.stack([real, imag])), "space", -2)
    ahead_real, ahead_imag = color_product(link_real, link_imag, upper[0], upper[1])
    back_real, back_imag = adjoint_product(link_real, link_imag, real, imag)
    lower = from_behind(for_sending(jnp.stack([back_real, back_imag])), "space", 2)
    total_real = total_real + ahead_real + lower[0]
    total_imag = total_imag + ahead_imag + lower[1]
    return (total_real, total_imag)


def pair_up(field):
    swapped = jnp.stack([field[:, :, 1], -field[:, :, 0]], axis=2)
    return jnp.concatenate([field, swapped], axis=1)


def project(left, right):
    left_flat = left.reshape(left.shape[0], left.shape[1], -1)
    right_flat = right.reshape(right.shape[0], right.shape[1], -1)
    return jnp.einsum("tkm,tvm->tkv", left_flat, right_flat, preferred_element_type=jnp.float32)


def local(solutions, links, eigvecs):
    slices = solutions.shape[0]
    vectors = solutions.shape[1]
    real = solutions[:, :, 0].reshape(slices, vectors, 3, -1)
    imag = solutions[:, :, 1].reshape(slices, vectors, 3, -1)
    link_flat = links.reshape(links.shape[:5] + (-1,))
    for step in range(NSMEAR):
        hop_real, hop_imag = hopping(real, imag, link_flat)
        real = real + kappa_hop * (hop_real - 6.0 * real)
        imag = imag + kappa_hop * (hop_imag - 6.0 * imag)
    smeared = jnp.stack([real, imag], axis=2).reshape(solutions.shape).astype(jnp.bfloat16)
    coefficients = project(eigvecs, pair_up(lax.all_gather(smeared, "space", axis=4, tiled=True)))
    return (smeared, coefficients)


def solution(mesh):
    placed = (
        P(("cfg", "tm"), None, None, None, "space", None),
        P(("cfg", "tm"), None, None, None, None, "space", None),
        P(("cfg", "tm"), "space", None, None, None, None),
    )
    return jax.shard_map(
        local,
        mesh=mesh,
        in_specs=placed,
        out_specs=(
            P(("cfg", "tm"), None, None, None, "space", None),
            P(("cfg", "tm"), "space", None),
        ),
        check_vma=False,
    )
```

profile of v0, /device:TPU:0, one launch (start us, length us, event | category | flops | bytes accessed | tf_op | source)
XLA Modules:
  0.0 97.3 jit_solution(8568620442478828379)
XLA Ops:
  0.6 1.1 %fusion.255 = (f32[1,4,1,3,1,2048]{5,4,3,2,1,0:T(1,128)S(1)}, f32[1,4,1,3,1,2048]{5,4,3,2,1,0:T(1,128)S(1)}) fusion(f32[1,4,2,3,1,2048]{5,4,3,2,1,0:T(1,128)} %param.3), kind=kLoop, calls=%fused_computation.622 | loop fusion | bytes 393216 | tf_op jit(solution)/shard_map/slice | solution.py:120
  1.9 5.1 %collective-permute-start.1 = (bf16[2,1,4,3,2048]{4,2,3,1,0:T(4,128)(2,1)S(1)}, bf16[2,1,4,3,2048]{4,2,3,1,0:T(4,128)(2,1)S(1)}, u32[]{:S(2)}, u32[]{:S(2)}) collective-permute-start(bf16[2,1,4,3,2048]{4,2,3,1,0:T(4,128)(2,1)S(1)} %pad_maximum_fusion), channel_id=1, source_target_pairs={{4,0},{6,2},{8,4},{10,6},{12,8},{14,10},{0,12},{2,14},{5,1},{7,3},... | collective-permute-start | bytes 294920 | tf_op jit(solution)/shard_map/ppermute | solution.py:34
  7.1 1.2 %negate_bitcast_fusion = (f32[1,3,3,2048]{3,0,1,2:T(1,128)S(1)}, f32[1,3,3,2048]{3,0,1,2:T(1,128)S(1)}, f32[1,3,3,2048]{3,0,1,2:T(1,128)S(1)}) fusion(f32[1,3,2,3,3,2048]{5,0,4,3,2,1:T(1,128)} %bitcast.1130), kind=kLoop, calls=%fused_computation.293 | loop fusion | flops 55296 | bytes 442368 | tf_op jit(solution)/shard_map/neg | solution.py:58
  8.3 1.3 %slice_bitcast_fusion.19 = (f32[1,3,3,2048]{3,0,1,2:T(1,128)S(1)}, f32[1,3,3,2048]{3,0,1,2:T(1,128)S(1)}, f32[1,3,3,2048]{3,0,1,2:T(1,128)S(1)}, f32[1,3,3,2048]...) fusion(f32[1,3,2,3,3,2048]{5,0,4,3,2,1:T(1,128)} %bitcast.1131), kind=kLoop, calls=%fused_computation.316 | loop fusion | bytes 1105920 | tf_op jit(solution)/shard_map/transpose | solution.py:58
  9.8 0.2 fusion.167
  10.4 0.3 subtract_add_fusion.7
  10.9 1.6 %collective-permute-start = (f32[4,1,4,3,64]{4,2,3,1,0:T(4,128)S(1)}, f32[4,1,4,3,64]{4,2,3,1,0:T(4,128)S(1)}, u32[]{:S(2)}, u32[]{:S(2)}) collective-permute-start(f32[4,1,4,3,64]{4,2,3,1,0:T(4,128)S(1)} %pad_maximum_fusion.17), channel_id=1, source_target_pairs={{0,2},{2,0},{4,6},{6,4},{8,10},{10,8},{12,14},{14,12},{1,3},{3,1},... | collective-permute-start | bytes 36872 | tf_op jit(solution)/shard_map/ppermute | solution.py:20
  13.5 0.2 maximum_select_fusion
  14.4 0.4 collective-permute-done
  15.0 1.5 %collective-permute-done.2 = bf16[2,1,4,3,2048]{4,2,3,1,0:T(4,128)(2,1)S(1)} collective-permute-done((bf16[2,1,4,3,2048]{4,2,3,1,0:T(4,128)(2,1)S(1)}, bf16[2,1,4,3,2048]{4,2,3,1,0:T(4,128)(2,1)S(1)}, u32[]{:S(2)}, u32[]{:S(2)}) %collective-permute-start.2) | collective-permute-done | bytes 98336 | tf_op jit(solution)/shard_map/ppermute | solution.py:34
  16.5 0.5 fusion.16
  17.4 0.5 fusion.23
  18.3 0.2 fusion.169
  18.4 0.3 subtract_add_fusion.5
  19.5 0.2 maximum_select_fusion.4
  19.9 1.6 %collective-permute-start.3 = (f32[4,1,4,3,64]{4,2,3,1,0:T(4,128)S(1)}, f32[4,1,4,3,64]{4,2,3,1,0:T(4,128)S(1)}, u32[]{:S(2)}, u32[]{:S(2)}) collective-permute-start(f32[4,1,4,3,64]{4,2,3,1,0:T(4,128)S(1)} %pad_maximum_fusion.18), channel_id=1, source_target_pairs={{0,2},{2,0},{4,6},{6,4},{8,10},{10,8},{12,14},{14,12},{1,3},{3,1},... | collective-permute-start | bytes 36872 | tf_op jit(solution)/shard_map/ppermute | solution.py:20
  21.5 0.5 fusion.250
  22.0 0.5 fusion.252
  22.6 3.9 %collective-permute-start.4 = (bf16[2,1,4,3,2048]{4,2,3,1,0:T(4,128)(2,1)S(1)}, bf16[2,1,4,3,2048]{4,2,3,1,0:T(4,128)(2,1)S(1)}, u32[]{:S(2)}, u32[]{:S(2)}) collective-permute-start(bf16[2,1,4,3,2048]{4,2,3,1,0:T(4,128)(2,1)S(1)} %pad_maximum_fusion.2), channel_id=1, source_target_pairs={{4,0},{6,2},{8,4},{10,6},{12,8},{14,10},{0,12},{2,14},{5,1},{7,3},... | collective-permute-start | bytes 294920 | tf_op jit(solution)/shard_map/ppermute | solution.py:34
  26.6 2.0 %collective-permute-done.4 = bf16[2,1,4,3,2048]{4,2,3,1,0:T(4,128)(2,1)S(1)} collective-permute-done((bf16[2,1,4,3,2048]{4,2,3,1,0:T(4,128)(2,1)S(1)}, bf16[2,1,4,3,2048]{4,2,3,1,0:T(4,128)(2,1)S(1)}, u32[]{:S(2)}, u32[]{:S(2)}) %collective-permute-start.4) | collective-permute-done | bytes 98336 | tf_op jit(solution)/shard_map/ppermute | solution.py:34
  28.7 0.5 fusion.38
  29.6 0.5 fusion.45
  30.5 0.2 fusion.171
  30.7 0.3 subtract_add_fusion.3
  31.7 0.2 maximum_select_fusion.11
  32.0 0.2 collective-permute-start.8
  32.2 1.1 %collective-permute-start.6 = (f32[4,1,4,3,64]{4,2,3,1,0:T(4,128)S(1)}, f32[4,1,4,3,64]{4,2,3,1,0:T(4,128)S(1)}, u32[]{:S(2)}, u32[]{:S(2)}) collective-permute-start(f32[4,1,4,3,64]{4,2,3,1,0:T(4,128)S(1)} %pad_maximum_fusion.19), channel_id=1, source_target_pairs={{0,2},{2,0},{4,6},{6,4},{8,10},{10,8},{12,14},{14,12},{1,3},{3,1},... | collective-permute-start | bytes 36872 | tf_op jit(solution)/shard_map/ppermute | solution.py:20
  33.3 0.5 fusion.246
  33.8 0.5 fusion.248
  34.4 3.8 %collective-permute-start.7 = (bf16[2,1,4,3,2048]{4,2,3,1,0:T(4,128)(2,1)S(1)}, bf16[2,1,4,3,2048]{4,2,3,1,0:T(4,128)(2,1)S(1)}, u32[]{:S(2)}, u32[]{:S(2)}) collective-permute-start(bf16[2,1,4,3,2048]{4,2,3,1,0:T(4,128)(2,1)S(1)} %pad_maximum_fusion.4), channel_id=1, source_target_pairs={{4,0},{6,2},{8,4},{10,6},{12,8},{14,10},{0,12},{2,14},{5,1},{7,3},... | collective-permute-start | bytes 294920 | tf_op jit(solution)/shard_map/ppermute | solution.py:34
  38.4 2.0 %collective-permute-done.7 = bf16[2,1,4,3,2048]{4,2,3,1,0:T(4,128)(2,1)S(1)} collective-permute-done((bf16[2,1,4,3,2048]{4,2,3,1,0:T(4,128)(2,1)S(1)}, bf16[2,1,4,3,2048]{4,2,3,1,0:T(4,128)(2,1)S(1)}, u32[]{:S(2)}, u32[]{:S(2)}) %collective-permute-start.7) | collective-permute-done | bytes 98336 | tf_op jit(solution)/shard_map/ppermute | solution.py:34
  40.6 0.5 fusion.60
  41.4 0.5 fusion.68
  42.3 0.2 fusion.173
  42.5 0.3 subtract_add_fusion.1
  43.4 0.2 maximum_select_fusion.18
  43.6 1.6 %collective-permute-start.9 = (f32[4,1,4,3,64]{4,2,3,1,0:T(4,128)S(1)}, f32[4,1,4,3,64]{4,2,3,1,0:T(4,128)S(1)}, u32[]{:S(2)}, u32[]{:S(2)}) collective-permute-start(f32[4,1,4,3,64]{4,2,3,1,0:T(4,128)S(1)} %pad_maximum_fusion.20), channel_id=1, source_target_pairs={{0,2},{2,0},{4,6},{6,4},{8,10},{10,8},{12,14},{14,12},{1,3},{3,1},... | collective-permute-start | bytes 36872 | tf_op jit(solution)/shard_map/ppermute | solution.py:20
  45.2 1.5 %collective-permute-start.11 = (bf16[2,1,4,3,2048]{4,2,3,1,0:T(4,128)(2,1)S(1)}, bf16[2,1,4,3,2048]{4,2,3,1,0:T(4,128)(2,1)S(1)}, u32[]{:S(2)}, u32[]{:S(2)}) collective-permute-start(bf16[2,1,4,3,2048]{4,2,3,1,0:T(4,128)(2,1)S(1)} %pad_maximum_fusion.7), channel_id=1, source_target_pairs={{12,0},{14,2},{0,4},{2,6},{4,8},{6,10},{8,12},{10,14},{13,1},{15,3... | collective-permute-start | bytes 294920 | tf_op jit(solution)/shard_map/ppermute | solution.py:34
  46.8 0.5 fusion.64
  47.3 0.5 fusion.72
  47.9 2.8 %collective-permute-start.10 = (bf16[2,1,4,3,2048]{4,2,3,1,0:T(4,128)(2,1)S(1)}, bf16[2,1,4,3,2048]{4,2,3,1,0:T(4,128)(2,1)S(1)}, u32[]{:S(2)}, u32[]{:S(2)}) collective-permute-start(bf16[2,1,4,3,2048]{4,2,3,1,0:T(4,128)(2,1)S(1)} %pad_maximum_fusion.6), channel_id=1, source_target_pairs={{4,0},{6,2},{8,4},{10,6},{12,8},{14,10},{0,12},{2,14},{5,1},{7,3},... | collective-permute-start | bytes 294920 | tf_op jit(solution)/shard_map/ppermute | solution.py:34
  50.8 2.3 %collective-permute-done.10 = bf16[2,1,4,3,2048]{4,2,3,1,0:T(4,128)(2,1)S(1)} collective-permute-done((bf16[2,1,4,3,2048]{4,2,3,1,0:T(4,128)(2,1)S(1)}, bf16[2,1,4,3,2048]{4,2,3,1,0:T(4,128)(2,1)S(1)}, u32[]{:S(2)}, u32[]{:S(2)}) %collective-permute-start.10) | collective-permute-done | bytes 98336 | tf_op jit(solution)/shard_map/ppermute | solution.py:34
  53.2 2.9 %fusion.165 = bf16[1,4,1,3,2048]{4,1,3,2,0:T(4,128)(2,1)S(1)} fusion(f32[1,4,1,3,1984]{4,1,3,2,0:T(4,128)S(1)} %slice_bitcast_fusion, f32[1,4,1,3,64]{4,1,3,2,0:T(4,128)S(1)} %get-tuple-element.319, f32[1,4,1,3,2047]{4,1,3,2,0:T(4,128)S(1)} %slice_bitcast_fusion.1, f32[1,4,1,3,1]{4,1,3,2,0:T(4,128)S(1)} %slice_bitcast_fusion.98, ...), kind=kLoop, calls=%fused_computation.272 | loop fusion | flops 4644864 | bytes 4327424 | tf_op jit(solution)/shard_map/convert.39
  56.1 2.9 %fusion.166 = bf16[1,4,1,3,2048]{4,1,3,2,0:T(4,128)(2,1)S(1)} fusion(f32[1,4,1,3,1984]{4,1,3,2,0:T(4,128)S(1)} %slice_bitcast_fusion.3, f32[1,4,1,3,64]{4,1,3,2,0:T(4,128)S(1)} %get-tuple-element.318, f32[1,4,1,3,2047]{4,1,3,2,0:T(4,128)S(1)} %slice_bitcast_fusion.4, f32[1,4,1,3,1]{4,1,3,2,0:T(4,128)S(1)} %slice_bitcast_fusion.107, ...), kind=kLoop, calls=%fused_computation.273 | loop fusion | flops 4644864 | bytes 4327424 | tf_op jit(solution)/shard_map/convert.38
  59.1 0.7 copy.168
  59.8 32.5 %all-gather = bf16[1,4,2,3,16384]{4,1,3,2,0:T(4,128)(2,1)S(1)} all-gather(bf16[1,4,2,3,2048]{4,1,3,2,0:T(4,128)(2,1)S(1)} %get-tuple-element.86), channel_id=2, replica_groups=mesh['cfg'=2,'space'=8,'tm'=2] {'space'}, dimensions={4}, use_global_device_ids=true | all-gather | bytes 884736 | tf_op jit(solution)/shard_map/all_gather | solution.py:128
  92.3 0.3 fusion.254
  92.7 4.6 %fusion.6 = f32[1,16,8]{1,2,0:T(8,128)} fusion(bf16[16,2,3,8,2048]{4,3,2,1,0:T(8,128)(2,1)S(1)} %bitcast.867, bf16[1,4,1,3,8,2048]{5,1,4,3,2,0:T(4,128)(2,1)S(1)} %get-tuple-element.15, bf16[1,4,1,3,8,2048]{5,1,4,3,2,0:T(4,128)(2,1)S(1)} %get-tuple-element.14, bf16[1,4,2,3,8,2048]{5,1,4,3,2,0:T(4,128)(2,1)S(1)} %bitcast.1125), kind=kOutput, calls=%fused_computation.7 | convolution fusion | flops 29884416 | bytes 4719104 | tf_op jit(solution)/shard_map/tkm,tvm->tkv/dot_general | solution.py:114
  (196 shorter events, 7.7 us)
Async XLA Ops:
  0.6 92.0 %copy-start = (bf16[1,16,2,3,8,2048]{5,4,3,2,1,0:T(8,128)(2,1)S(1)}, bf16[1,16,2,3,8,2048]{5,4,3,2,1,0:T(8,128)(2,1)}, u32[]{:S(2)}) copy-start(bf16[1,16,2,3,8,2048]{5,4,3,2,1,0:T(8,128)(2,1)} %param.5) | copy-start | bytes 9437188
  1.9 13.0 %collective-permute-start.1 = (bf16[2,1,4,3,2048]{4,2,3,1,0:T(4,128)(2,1)S(1)}, bf16[2,1,4,3,2048]{4,2,3,1,0:T(4,128)(2,1)S(1)}, u32[]{:S(2)}, u32[]{:S(2)}) collective-permute-start(bf16[2,1,4,3,2048]{4,2,3,1,0:T(4,128)(2,1)S(1)} %pad_maximum_fusion), channel_id=1, source_target_pairs={{4,0},{6,2},{8,4},{10,6},{12,8},{14,10},{0,12},{2,14},{5,1},{7,3},... | collective-permute-start | bytes 294920 | tf_op jit(solution)/shard_map/ppermute | solution.py:34
  10.1 6.5 %collective-permute-start.2 = (bf16[2,1,4,3,2048]{4,2,3,1,0:T(4,128)(2,1)S(1)}, bf16[2,1,4,3,2048]{4,2,3,1,0:T(4,128)(2,1)S(1)}, u32[]{:S(2)}, u32[]{:S(2)}) collective-permute-start(bf16[2,1,4,3,2048]{4,2,3,1,0:T(4,128)(2,1)S(1)} %pad_maximum_fusion.1), channel_id=1, source_target_pairs={{12,0},{14,2},{0,4},{2,6},{4,8},{6,10},{8,12},{10,14},{13,1},{15,3... | collective-permute-start | bytes 294920 | tf_op jit(solution)/shard_map/ppermute | solution.py:34
  10.9 3.9 %collective-permute-start = (f32[4,1,4,3,64]{4,2,3,1,0:T(4,128)S(1)}, f32[4,1,4,3,64]{4,2,3,1,0:T(4,128)S(1)}, u32[]{:S(2)}, u32[]{:S(2)}) collective-permute-start(f32[4,1,4,3,64]{4,2,3,1,0:T(4,128)S(1)} %pad_maximum_fusion.17), channel_id=1, source_target_pairs={{0,2},{2,0},{4,6},{6,4},{8,10},{10,8},{12,14},{14,12},{1,3},{3,1},... | collective-permute-start | bytes 36872 | tf_op jit(solution)/shard_map/ppermute | solution.py:20
  19.8 8.9 %collective-permute-start.5 = (bf16[2,1,4,3,2048]{4,2,3,1,0:T(4,128)(2,1)S(1)}, bf16[2,1,4,3,2048]{4,2,3,1,0:T(4,128)(2,1)S(1)}, u32[]{:S(2)}, u32[]{:S(2)}) collective-permute-start(bf16[2,1,4,3,2048]{4,2,3,1,0:T(4,128)(2,1)S(1)} %pad_maximum_fusion.3), channel_id=1, source_target_pairs={{12,0},{14,2},{0,4},{2,6},{4,8},{6,10},{8,12},{10,14},{13,1},{15,3... | collective-permute-start | bytes 294920 | tf_op jit(solution)/shard_map/ppermute | solution.py:34
  19.9 6.5 %collective-permute-start.3 = (f32[4,1,4,3,64]{4,2,3,1,0:T(4,128)S(1)}, f32[4,1,4,3,64]{4,2,3,1,0:T(4,128)S(1)}, u32[]{:S(2)}, u32[]{:S(2)}) collective-permute-start(f32[4,1,4,3,64]{4,2,3,1,0:T(4,128)S(1)} %pad_maximum_fusion.18), channel_id=1, source_target_pairs={{0,2},{2,0},{4,6},{6,4},{8,10},{10,8},{12,14},{14,12},{1,3},{3,1},... | collective-permute-start | bytes 36872 | tf_op jit(solution)/shard_map/ppermute | solution.py:20
  22.6 6.1 %collective-permute-start.4 = (bf16[2,1,4,3,2048]{4,2,3,1,0:T(4,128)(2,1)S(1)}, bf16[2,1,4,3,2048]{4,2,3,1,0:T(4,128)(2,1)S(1)}, u32[]{:S(2)}, u32[]{:S(2)}) collective-permute-start(bf16[2,1,4,3,2048]{4,2,3,1,0:T(4,128)(2,1)S(1)} %pad_maximum_fusion.2), channel_id=1, source_target_pairs={{4,0},{6,2},{8,4},{10,6},{12,8},{14,10},{0,12},{2,14},{5,1},{7,3},... | collective-permute-start | bytes 294920 | tf_op jit(solution)/shard_map/ppermute | solution.py:34
  32.0 8.5 %collective-permute-start.8 = (bf16[2,1,4,3,2048]{4,2,3,1,0:T(4,128)(2,1)S(1)}, bf16[2,1,4,3,2048]{4,2,3,1,0:T(4,128)(2,1)S(1)}, u32[]{:S(2)}, u32[]{:S(2)}) collective-permute-start(bf16[2,1,4,3,2048]{4,2,3,1,0:T(4,128)(2,1)S(1)} %pad_maximum_fusion.5), channel_id=1, source_target_pairs={{12,0},{14,2},{0,4},{2,6},{4,8},{6,10},{8,12},{10,14},{13,1},{15,3... | collective-permute-start | bytes 294920 | tf_op jit(solution)/shard_map/ppermute | solution.py:34
  32.2 6.0 %collective-permute-start.6 = (f32[4,1,4,3,64]{4,2,3,1,0:T(4,128)S(1)}, f32[4,1,4,3,64]{4,2,3,1,0:T(4,128)S(1)}, u32[]{:S(2)}, u32[]{:S(2)}) collective-permute-start(f32[4,1,4,3,64]{4,2,3,1,0:T(4,128)S(1)} %pad_maximum_fusion.19), channel_id=1, source_target_pairs={{0,2},{2,0},{4,6},{6,4},{8,10},{10,8},{12,14},{14,12},{1,3},{3,1},... | collective-permute-start | bytes 36872 | tf_op jit(solution)/shard_map/ppermute | solution.py:20
  34.4 6.1 %collective-permute-start.7 = (bf16[2,1,4,3,2048]{4,2,3,1,0:T(4,128)(2,1)S(1)}, bf16[2,1,4,3,2048]{4,2,3,1,0:T(4,128)(2,1)S(1)}, u32[]{:S(2)}, u32[]{:S(2)}) collective-permute-start(bf16[2,1,4,3,2048]{4,2,3,1,0:T(4,128)(2,1)S(1)} %pad_maximum_fusion.4), channel_id=1, source_target_pairs={{4,0},{6,2},{8,4},{10,6},{12,8},{14,10},{0,12},{2,14},{5,1},{7,3},... | collective-permute-start | bytes 294920 | tf_op jit(solution)/shard_map/ppermute | solution.py:34
  43.6 7.1 %collective-permute-start.9 = (f32[4,1,4,3,64]{4,2,3,1,0:T(4,128)S(1)}, f32[4,1,4,3,64]{4,2,3,1,0:T(4,128)S(1)}, u32[]{:S(2)}, u32[]{:S(2)}) collective-permute-start(f32[4,1,4,3,64]{4,2,3,1,0:T(4,128)S(1)} %pad_maximum_fusion.20), channel_id=1, source_target_pairs={{0,2},{2,0},{4,6},{6,4},{8,10},{10,8},{12,14},{14,12},{1,3},{3,1},... | collective-permute-start | bytes 36872 | tf_op jit(solution)/shard_map/ppermute | solution.py:20
  45.2 8.0 %collective-permute-start.11 = (bf16[2,1,4,3,2048]{4,2,3,1,0:T(4,128)(2,1)S(1)}, bf16[2,1,4,3,2048]{4,2,3,1,0:T(4,128)(2,1)S(1)}, u32[]{:S(2)}, u32[]{:S(2)}) collective-permute-start(bf16[2,1,4,3,2048]{4,2,3,1,0:T(4,128)(2,1)S(1)} %pad_maximum_fusion.7), channel_id=1, source_target_pairs={{12,0},{14,2},{0,4},{2,6},{4,8},{6,10},{8,12},{10,14},{13,1},{15,3... | collective-permute-start | bytes 294920 | tf_op jit(solution)/shard_map/ppermute | solution.py:34
  47.9 5.3 %collective-permute-start.10 = (bf16[2,1,4,3,2048]{4,2,3,1,0:T(4,128)(2,1)S(1)}, bf16[2,1,4,3,2048]{4,2,3,1,0:T(4,128)(2,1)S(1)}, u32[]{:S(2)}, u32[]{:S(2)}) collective-permute-start(bf16[2,1,4,3,2048]{4,2,3,1,0:T(4,128)(2,1)S(1)} %pad_maximum_fusion.6), channel_id=1, source_target_pairs={{4,0},{6,2},{8,4},{10,6},{12,8},{14,10},{0,12},{2,14},{5,1},{7,3},... | collective-permute-start | bytes 294920 | tf_op jit(solution)/shard_map/ppermute | solution.py:34
where the time goes:
time: 97.5 us; the launch traced here: 97.3 us
  blocking collectives  32.5 us (33%)
  starting transfers between devices  23.2 us (24%)
  other arithmetic  17.3 us (18%)
  local copies, waits for them, and re-layouts  9.41 us (10%)
  waiting for transfers between devices  8.32 us (9%)
  matrix products  4.62 us (5%)
  between operations  1.87 us (2%)
    all_gather x1, blocking collectives, local(): lax.all_gather(smeared, 'space', axis=4, tiled=True)  32.5 us
    ppermute x8, starting transfers between devices, from_behind(): return lax.ppermute(block, axis, route)  17.5 us
    another operation x8, other arithmetic  8.81 us
    ppermute x8, waiting for transfers between devices, from_behind(): return lax.ppermute(block, axis, route)  7.92 us
    ppermute x4, starting transfers between devices, swapped_2(): return lax.ppermute(block, axis, route)  5.72 us
    dot_general x1, matrix products, project(): jnp.einsum('tkm,tvm->tkv', left_flat, right_flat, preferred_element_type=...  4.62 us
  transfers between devices with their start and end apart: 12, of which 5 were waited for; matrix products, arithmetic and copies ran while one was open for 10% of the time, Pallas kernels for 0%

commit v1 on v0

--- a/solution.py
+++ b/solution.py
@@ -1,6 +1,9 @@
 import jax
 import jax.numpy as jnp
+import numpy as np
 from jax import lax
+from jax.experimental import pallas as pl
+from jax.experimental.pallas import tpu as pltpu
 from jax.sharding import PartitionSpec as P
 
 NSMEAR = 4
@@ -114,7 +117,7 @@
     return jnp.einsum("tkm,tvm->tkv", left_flat, right_flat, preferred_element_type=jnp.float32)
 
 
-def local(solutions, links, eigvecs):
+def by_planes(solutions, links, eigvecs):
     slices = solutions.shape[0]
     vectors = solutions.shape[1]
     real = solutions[:, :, 0].reshape(slices, vectors, 3, -1)
@@ -129,6 +132,260 @@
     return (smeared, coefficients)
 
 
+PLANES = 4
+FIELDS = 24
+LINKS = 54
+PARTS = FIELDS + LINKS
+WINDOW = PARTS * 8
+
+
+def is_diagonal(part):
+    return part % 18 in (0, 4, 8)
+
+
+def pack_kernel(place, field, link, edges, *rest):
+    outs, wide, windows, narrow = rest[:PLANES], rest[PLANES], rest[PLANES + 1], rest[PLANES + 2]
+    z = place[0]
+    h = place[1]
+    wide[:FIELDS, 2:18, :] = field[...]
+    for part in range(LINKS):
+        entry = link[part]
+        wide[FIELDS + part, 2:18, :] = entry - 1.0 if is_diagonal(part) else entry
+    narrow[...] = edges[...].astype(jnp.float32)
+    for part in range(PARTS):
+        wide[part, 18:20, :] = narrow[4 * part : 4 * part + 2, :]
+        wide[part, 0:2, :] = narrow[4 * part + 2 : 4 * part + 4, :]
+    for slab in range(PLANES):
+        window = wide[:, 4 * slab : 4 * slab + 8, :]
+        windows[slab] = window.reshape(WINDOW, 128).astype(jnp.bfloat16)
+    for hop in range(PLANES):
+        target = lax.rem(z + hop, PLANES)
+        slab = jnp.where(h == 0, target, PLANES - 1 - target)
+        outs[hop][...] = windows[slab]
+
+
+def apply_links(matrix, field):
+    out = []
+    for row in range(3):
+        real = imag = None
+        for inner in range(3):
+            re, im = matrix(row, inner)
+            term_real = re * field[inner] - im * field[3 + inner]
+            term_imag = re * field[3 + inner] + im * field[inner]
+            real = term_real if real is None else real + term_real
+            imag = term_imag if imag is None else imag + term_imag
+        out.append((real, imag))
+    return [pair[0] for pair in out] + [pair[1] for pair in out]
+
+
+def smear_kernel(place, *rest):
+    blocks, out = rest[:PLANES], rest[PLANES]
+    phi, links, flat = rest[PLANES + 1 :]
+    lane = lax.broadcasted_iota(jnp.int32, (8, 128), 1)
+    x_place = lane % LX
+    at_end = x_place == LX - 1
+    at_start = x_place == 0
+    low = lane < LX
+
+    for plane in range(PLANES):
+        values = blocks[plane][...].astype(jnp.float32).reshape(PARTS, 8, 128)
+        phi[0, plane] = values[:FIELDS]
+        for part in range(LINKS):
+            entry = values[FIELDS + part]
+            links[plane, part] = kappa_hop * (entry + 1.0 if is_diagonal(part) else entry)
+
+    def next_x(a):
+        return jnp.where(at_end, pltpu.roll(a, LX - 1, 1), pltpu.roll(a, 127, 1))
+
+    def last_x(a):
+        return jnp.where(at_start, pltpu.roll(a, LX + 1, 1), pltpu.roll(a, 1, 1))
+
+    def next_y(a):
+        other = pltpu.roll(a, LX, 1)
+        return jnp.where(low, other, pltpu.roll(other, 7, 0))
+
+    def last_y(a):
+        other = pltpu.roll(a, LX, 1)
+        return jnp.where(low, pltpu.roll(other, 1, 0), other)
+
+    def forward(plane, along):
+        def entry(row, inner):
+            at = along * 18 + row * 3 + inner
+            return links[plane, at], links[plane, at + 9]
+
+        return entry
+
+    def backward(plane, along):
+        def entry(row, inner):
+            at = along * 18 + inner * 3 + row
+            return links[plane, at], -links[plane, at + 9]
+
+        return entry
+
+    def one_step(source, target):
+        def one(index, carry):
+            plane = index // 2
+            pair = index % 2
+            above = lax.rem(plane + 3, PLANES)
+            below = lax.rem(plane + 1, PLANES)
+            for vector in range(2):
+                base = (pair * 2 + vector) * 6
+                field = [phi[source, plane, base + i] for i in range(6)]
+                upper = [phi[source, above, base + i] for i in range(6)]
+                lower = [phi[source, below, base + i] for i in range(6)]
+                total = [(1.0 - 6.0 * kappa_hop) * a for a in field]
+
+                def add(terms):
+                    for i in range(6):
+                        total[i] = total[i] + terms[i]
+
+                add(apply_links(forward(plane, 0), [next_x(a) for a in field]))
+                add([last_x(a) for a in apply_links(backward(plane, 0), field)])
+                add(apply_links(forward(plane, 1), [next_y(a) for a in field]))
+                add([last_y(a) for a in apply_links(backward(plane, 1), field)])
+                add(apply_links(forward(plane, 2), upper))
+                add(apply_links(backward(below, 2), lower))
+                for i in range(6):
+                    phi[target, plane, base + i] = total[i]
+            return carry
+
+        lax.fori_loop(0, 2 * PLANES, one, 0)
+
+    for step in range(NSMEAR):
+        one_step(step % 2, (step + 1) % 2)
+
+    last = NSMEAR % 2
+    for plane in range(PLANES):
+        true_plane = lax.rem(place[0] + PLANES - plane, PLANES)
+        for row in range(4):
+            flat[true_plane, :, row * 128 : (row + 1) * 128] = phi[last, plane, :, 2 + row, :]
+    out[...] = flat[...].reshape(PLANES * FIELDS, 512).astype(jnp.bfloat16)
+
+
+def project_kernel(place, eigvecs, masks, *rest):
+    own, other = rest[:PLANES], rest[PLANES : 2 * PLANES]
+    smeared, coefficients, sites, column = rest[2 * PLANES :]
+    z = place[0]
+    h = place[1]
+    half = PLANES * FIELDS
+    for hop in range(PLANES):
+        origin = lax.rem(z + PLANES - hop, PLANES)
+        for blocks, side in ((own, h), (other, 1 - h)):
+            slab = jnp.where(side == 0, origin, PLANES - 1 - origin)
+            rows = pl.ds(pl.multiple_of(side * half, half), half)
+            columns = pl.ds(pl.multiple_of(slab * 512, 512), 512)
+            sites[rows, columns] = blocks[hop][...]
+            if blocks is own:
+                wide = blocks[hop][...].astype(jnp.float32)
+                column[:, :, columns] = wide.reshape(PLANES, FIELDS, 512)
+    smeared[...] = column[z].astype(jnp.bfloat16)
+    vector = masks[96:97, :]
+    count = 4
+    for group in range(eigvecs.shape[0] // (48 * count)):
+        rows = eigvecs[group * 48 * count : (group + 1) * 48 * count, :]
+        product = lax.dot_general(
+            rows, sites[...], (((1,), (1,)), ((), ())), preferred_element_type=jnp.float32
+        ).reshape(count, 48, 2 * half)
+        for at, mask in ((0, masks[0:48, :]), (4, masks[48:96, :])):
+            sums = jnp.sum(product * mask[None], axis=1)
+            for v in range(4):
+                picked = jnp.where(vector == float(v), sums, 0.0)
+                coefficients[group * count : (group + 1) * count, at + v : at + v + 1] = jnp.sum(
+                    picked, axis=1, keepdims=True
+                )
+
+
+def projection_masks():
+    row = np.arange(48)[:, None]
+    ri, color, r = row // 24, row // 8 % 3, row % 8
+    column = np.arange(192)[None]
+    h, z, v = column // 96, column // 24 % 4, column // 6 % 4
+    ri_right, color_right = column // 3 % 2, column % 3
+    here = (color == color_right) & (r == 2 * z + h)
+    real = np.where(here & (ri == ri_right), 1.0, 0.0)
+    imag = np.where(here & (ri != ri_right), np.where(ri == 0, 1.0, -1.0), 0.0)
+    vectors = np.broadcast_to(v, (8, 192))
+    return np.concatenate([real, imag, vectors]).astype(np.float32)
+
+
+def on_device(count):
+    return [pl.BlockSpec(memory_space=pltpu.VMEM)] * count
+
+
+def in_slabs(solutions, links, eigvecs):
+    me = lax.axis_index("space")
+    place = jnp.stack([me // 2, me % 2]).astype(jnp.int32)
+    scalars = [pl.BlockSpec(memory_space=pltpu.SMEM)]
+    limit = pltpu.CompilerParams(vmem_limit_bytes=32 * 1024 * 1024)
+
+    def swapped(block):
+        return lax.ppermute(block, "space", [(i, i ^ 1) for i in range(2 * PLANES)])
+
+    def moved_up(block, planes):
+        count = 2 * PLANES
+        return lax.ppermute(block, "space", [(i, (i + 2 * planes) % count) for i in range(count)])
+
+    field = solutions.reshape(FIELDS, 16, 128)
+    link = links.reshape(LINKS, 16, 128)
+    unit = np.array([1.0 if is_diagonal(part) else 0.0 for part in range(LINKS)], np.float32)
+    both = jnp.concatenate([field, link - unit[:, None, None]])
+    edges = jnp.concatenate([both[:, 0:2], both[:, 14:16]], axis=1).astype(jnp.bfloat16)
+    edges = swapped(edges.reshape(4 * PARTS, 128))
+    window = jax.ShapeDtypeStruct((WINDOW, 128), jnp.bfloat16)
+    windows = pl.pallas_call(
+        pack_kernel,
+        out_shape=[window] * PLANES,
+        in_specs=scalars + on_device(3),
+        out_specs=on_device(PLANES),
+        scratch_shapes=[
+            pltpu.VMEM((PARTS, 24, 128), jnp.float32),
+            pltpu.VMEM((PLANES, WINDOW, 128), jnp.bfloat16),
+            pltpu.VMEM((4 * PARTS, 128), jnp.float32),
+        ],
+        compiler_params=limit,
+        name="pack",
+    )(place, field, link, edges)
+    blocks = [windows[0]] + [moved_up(windows[hop], hop) for hop in range(1, PLANES)]
+    block = pl.pallas_call(
+        smear_kernel,
+        out_shape=jax.ShapeDtypeStruct((PLANES * FIELDS, 512), jnp.bfloat16),
+        in_specs=scalars + on_device(PLANES),
+        out_specs=pl.BlockSpec(memory_space=pltpu.VMEM),
+        scratch_shapes=[
+            pltpu.VMEM((2, PLANES, FIELDS, 8, 128), jnp.float32),
+            pltpu.VMEM((PLANES, LINKS, 8, 128), jnp.float32),
+            pltpu.VMEM((PLANES, FIELDS, 512), jnp.float32),
+        ],
+        compiler_params=limit,
+        name="smear",
+    )(place, *blocks)
+    own = [block] + [moved_up(block, hop) for hop in range(1, PLANES)]
+    other = [swapped(part) for part in own]
+    vectors = eigvecs.shape[1]
+    smeared, coefficients = pl.pallas_call(
+        project_kernel,
+        out_shape=[
+            jax.ShapeDtypeStruct((FIELDS, 2048), jnp.bfloat16),
+            jax.ShapeDtypeStruct((vectors, 8), jnp.float32),
+        ],
+        in_specs=scalars + on_device(2 + 2 * PLANES),
+        out_specs=on_device(2),
+        scratch_shapes=[
+            pltpu.VMEM((2 * PLANES * FIELDS, 2048), jnp.bfloat16),
+            pltpu.VMEM((PLANES, FIELDS, 2048), jnp.float32),
+        ],
+        compiler_params=limit,
+        name="project",
+    )(place, eigvecs.reshape(vectors * 48, 2048), projection_masks(), *own, *other)
+    return smeared.reshape(solutions.shape), coefficients[None]
+
+
+def local(solutions, links, eigvecs):
+    fits = lax.axis_size("space") == 2 * PLANES and solutions.shape[:2] == (1, 4)
+    fits = fits and solutions.shape[4:] == (1, 2048) and eigvecs.shape[1] % 4 == 0
+    return (in_slabs if fits else by_planes)(solutions, links, eigvecs)
+
+
 def solution(mesh):
     placed = (
         P(("cfg", "tm"), None, None, None, "space", None),

time: 97.5 us -> 58.2 us (0.60)
  blocking collectives: 32.5 us -> 0 us
  other arithmetic: 17.3 us -> 2.31 us
  waiting for transfers between devices: 8.32 us -> 20.2 us
  Pallas kernels: 0 us -> 8.68 us
  matrix products: 4.62 us -> 0 us
  starting transfers between devices: 23.2 us -> 19.8 us
  local copies, waits for them, and re-layouts: 9.41 us -> 6.22 us
  between operations: 1.87 us -> 0.69 us
    all_gather x1 -> x0, blocking collectives: 32.5 us -> none  [local(): lax.all_gather(smeared, 'space', axis=4, tiled=True)]
    ppermute x12 -> x11, waiting for transfers between devices: 8.32 us -> 20.2 us  [the longest x6 13.8 us: moved_up(): lax.ppermute(block, 'space', [(i, (i + 2 * planes) % count) for i in rang...]
    another operation x25 -> x1, other arithmetic: 10.1 us -> 0.07 us  [in_slabs(): place = jnp.stack([me // 2, me % 2]).astype(jnp.int32)]
    pallas_call x0 -> x3, Pallas kernels: none -> 8.68 us  [the longest x1 6.08 us: in_slabs(): pl.pallas_call(smear_kernel, out_shape=jax.ShapeDtypeStruct((PLANES * FIE...]
    dot_general x1 -> x0, matrix products: 4.62 us -> none  [project(): jnp.einsum('tkm,tvm->tkv', left_flat, right_flat, preferred_element_type=...]
    add x10 -> x0, other arithmetic: 4.31 us -> none  [the longest x3 1.59 us: local(): imag = imag + kappa_hop * (hop_imag - 6.0 * imag)]
    unnamed x36 -> x9, local copies, waits for them, and re-layouts: 1.29 us -> 5.48 us
    slice x40 -> x0, local copies, waits for them, and re-layouts: 3.59 us -> none  [the longest x1 1.11 us: local(): real = solutions[:, :, 0].reshape(slices, vectors, 3, -1)]
  transfers between devices with their start and end apart: 12 -> 11, of which waited for: 5 -> 7; matrix products, arithmetic and copies ran while one was open for 10% -> 0% of each run, Pallas kernels for 0% -> 0%
where the time goes in v1:
time: 58.2 us; the launch traced here: 57.9 us
  waiting for transfers between devices  20.2 us (35%)
  starting transfers between devices  19.8 us (34%)
  Pallas kernels  8.68 us (15%)
  local copies, waits for them, and re-layouts  6.22 us (11%)
  other arithmetic  2.31 us (4%)
  between operations  0.69 us (1%)
    ppermute x6, waiting for transfers between devices, moved_up(): lax.ppermute(block, 'space', [(i, (i + 2 * planes) % count) for i in rang...  13.8 us
    ppermute x6, starting transfers between devices, moved_up(): lax.ppermute(block, 'space', [(i, (i + 2 * planes) % count) for i in rang...  11.7 us
    ppermute x5, starting transfers between devices, swapped(): return lax.ppermute(block, 'space', [(i, i ^ 1) for i in range(2 * PLANES)])  8.04 us
    ppermute x5, waiting for transfers between devices, swapped(): return lax.ppermute(block, 'space', [(i, i ^ 1) for i in range(2 * PLANES)])  6.41 us
    pallas_call x1, Pallas kernels, in_slabs(): pl.pallas_call(smear_kernel, out_shape=jax.ShapeDtypeStruct((PLANES * FIE...  6.08 us
    unnamed x9, local copies, waits for them, and re-layouts  5.48 us
    pallas_call x1, Pallas kernels, in_slabs(): pl.pallas_call(project_kernel, out_shape=[jax.ShapeDtypeStruct((FIELDS, 2...  1.86 us
  transfers between devices with their start and end apart: 11, of which 7 were waited for; matrix products, arithmetic and copies ran while one was open for 0% of the time, Pallas kernels for 0%

profile of v1, /device:TPU:0, one launch (start us, length us, event | category | flops | bytes accessed | tf_op | source)
XLA Modules:
  0.0 57.9 jit_solution(10010160614109331990)
XLA Ops:
  0.6 1.1 %broadcast_add_fusion = bf16[54,16,128]{2,1,0:T(8,128)(2,1)S(1)} fusion(f32[54,16,128]{2,1,0:T(8,128)} %bitcast.8, f32[54]{0:T(128)} %constant.40), kind=kLoop, calls=%fused_computation | loop fusion | flops 221184 | bytes 663768 | tf_op jit(solution)/shard_map/sub | solution.py:331
  1.8 1.0 %maximum_convert_fusion = (bf16[78,2,128]{2,1,0:T(2,128)(2,1)S(1)}, bf16[78,2,128]{2,1,0:T(2,128)(2,1)S(1)}) fusion(bf16[54,16,128]{2,1,0:T(8,128)(2,1)S(1)} %broadcast_add_fusion, f32[24,16,128]{2,1,0:T(8,128)} %bitcast.10), kind=kLoop, calls=%fused_computation.3 | loop fusion | flops 159744 | bytes 497664 | tf_op jit(solution)/shard_map/slice | solution.py:332
  2.8 0.1 pad_maximum_fusion.1
  2.9 3.0 %collective-permute-start = (bf16[312,128]{1,0:T(8,128)(2,1)S(1)}, bf16[312,128]{1,0:T(8,128)(2,1)S(1)}, u32[]{:S(2)}, u32[]{:S(2)}) collective-permute-start(bf16[312,128]{1,0:T(8,128)(2,1)S(1)} %bitcast.12), channel_id=1, source_target_pairs={{0,2},{2,0},{4,6},{6,4},{8,10},{10,8},{12,14},{14,12},{1,3},{3,1},... | collective-permute-start | bytes 239624 | tf_op jit(solution)/shard_map/ppermute | solution.py:322
  5.9 0.1 pad_add_fusion.place
  6.0 2.3 %collective-permute-done.edges = bf16[312,128]{1,0:T(8,128)(2,1)S(1)} collective-permute-done((bf16[312,128]{1,0:T(8,128)(2,1)S(1)}, bf16[312,128]{1,0:T(8,128)(2,1)S(1)}, u32[]{:S(2)}, u32[]{:S(2)}) %collective-permute-start) | collective-permute-done | bytes 79904 | tf_op jit(solution)/shard_map/ppermute | solution.py:322
  8.3 0.0 copy-start.1
  8.3 1.0 %copy-done.1 = f32[1,3,2,3,3,1,2048]{6,5,4,3,2,1,0:T(1,128)S(1)} copy-done((f32[1,3,2,3,3,1,2048]{6,5,4,3,2,1,0:T(1,128)S(1)}, f32[1,3,2,3,3,1,2048]{6,5,4,3,2,1,0:T(1,128)}, u32[]{:S(2)}) %copy-start.1) | copy-done | bytes 442392
  9.3 0.0 copy-start.2
  9.3 0.9 %copy-done.2 = f32[1,4,2,3,1,2048]{5,4,3,2,1,0:T(1,128)S(1)} copy-done((f32[1,4,2,3,1,2048]{5,4,3,2,1,0:T(1,128)S(1)}, f32[1,4,2,3,1,2048]{5,4,3,2,1,0:T(1,128)}, u32[]{:S(2)}) %copy-start.2) | copy-done | bytes 196632
  10.2 0.7 %pack.1 = (bf16[624,128]{1,0:T(8,128)(2,1)S(1)}, bf16[624,128]{1,0:T(8,128)(2,1)S(1)}, bf16[624,128]{1,0:T(8,128)(2,1)S(1)}, bf16[624,128]{1,0:T(8,128)(2,1)S(1)}) custom-call(s32[2]{0:T(128)S(1)} %pad_add_fusion.place, f32[24,16,128]{2,1,0:T(8,128)S(1)} %bitcast.11, f32[54,16,128]{2,1,0:T(8,128)S(1)} %bitcast.9, bf16[312,128]{1,0:T(8,128)(2,1)S(1)} %collective-permute-done.edges), custom_call_target="tpu_custom_call" | custom-call | tf_op jit(solution)/shard_map/pack/pallas_call | solution.py:335
  11.0 2.2 %collective-permute-start.1 = (bf16[624,128]{1,0:T(8,128)(2,1)S(1)}, bf16[624,128]{1,0:T(8,128)(2,1)S(1)}, u32[]{:S(2)}, u32[]{:S(2)}) collective-permute-start(bf16[624,128]{1,0:T(8,128)(2,1)S(1)} %get-tuple-element.9), channel_id=1, source_target_pairs={{0,4},{2,6},{4,8},{6,10},{8,12},{10,14},{12,0},{14,2},{1,5},{3,7},... | collective-permute-start | bytes 479240 | tf_op jit(solution)/shard_map/ppermute | solution.py:326
  13.1 2.6 %collective-permute-start.2 = (bf16[624,128]{1,0:T(8,128)(2,1)S(1)}, bf16[624,128]{1,0:T(8,128)(2,1)S(1)}, u32[]{:S(2)}, u32[]{:S(2)}) collective-permute-start(bf16[624,128]{1,0:T(8,128)(2,1)S(1)} %get-tuple-element.10), channel_id=1, source_target_pairs={{0,8},{2,10},{4,12},{6,14},{8,0},{10,2},{12,4},{14,6},{1,9},{3,11}... | collective-permute-start | bytes 479240 | tf_op jit(solution)/shard_map/ppermute | solution.py:326
  15.7 1.3 %collective-permute-start.3 = (bf16[624,128]{1,0:T(8,128)(2,1)S(1)}, bf16[624,128]{1,0:T(8,128)(2,1)S(1)}, u32[]{:S(2)}, u32[]{:S(2)}) collective-permute-start(bf16[624,128]{1,0:T(8,128)(2,1)S(1)} %get-tuple-element.11), channel_id=1, source_target_pairs={{0,12},{2,14},{4,0},{6,2},{8,4},{10,6},{12,8},{14,10},{1,13},{3,15... | collective-permute-start | bytes 479240 | tf_op jit(solution)/shard_map/ppermute | solution.py:326
  17.1 3.2 %collective-permute-done.1.rest_1_ = bf16[624,128]{1,0:T(8,128)(2,1)S(1)} collective-permute-done((bf16[624,128]{1,0:T(8,128)(2,1)S(1)}, bf16[624,128]{1,0:T(8,128)(2,1)S(1)}, u32[]{:S(2)}, u32[]{:S(2)}) %collective-permute-start.1) | collective-permute-done | bytes 159776 | tf_op jit(solution)/shard_map/ppermute | solution.py:326
  20.3 4.8 %collective-permute-done.2.rest_2_ = bf16[624,128]{1,0:T(8,128)(2,1)S(1)} collective-permute-done((bf16[624,128]{1,0:T(8,128)(2,1)S(1)}, bf16[624,128]{1,0:T(8,128)(2,1)S(1)}, u32[]{:S(2)}, u32[]{:S(2)}) %collective-permute-start.2) | collective-permute-done | bytes 159776 | tf_op jit(solution)/shard_map/ppermute | solution.py:326
  25.1 0.0 collective-permute-done.3.rest_3_
  25.1 6.1 %smear.1.rest_0_ = bf16[96,512]{1,0:T(8,128)(2,1)S(1)} custom-call(s32[2]{0:T(128)S(1)} %pad_add_fusion.place, bf16[624,128]{1,0:T(8,128)(2,1)S(1)} %get-tuple-element.8.rest_0_, bf16[624,128]{1,0:T(8,128)(2,1)S(1)} %collective-permute-done.1.rest_1_, bf16[624,128]{1,0:T(8,128)(2,1)S(1)} %collective-permute-done.2.rest_2_, ...), custom_call_target="tpu_custom_call" | custom-call | tf_op jit(solution)/shard_map/smear/pallas_call | solution.py:349
  31.2 5.0 %collective-permute-start.6 = (bf16[96,512]{1,0:T(8,128)(2,1)S(1)}, bf16[96,512]{1,0:T(8,128)(2,1)S(1)}, u32[]{:S(2)}, u32[]{:S(2)}) collective-permute-start(bf16[96,512]{1,0:T(8,128)(2,1)S(1)} %smear.1.rest_0_), channel_id=1, source_target_pairs={{0,12},{2,14},{4,0},{6,2},{8,4},{10,6},{12,8},{14,10},{1,13},{3,15... | collective-permute-start | bytes 294920 | tf_op jit(solution)/shard_map/ppermute | solution.py:326
  36.2 0.4 collective-permute-start.5
  36.6 0.2 collective-permute-start.4
  36.8 1.5 %collective-permute-start.7 = (bf16[96,512]{1,0:T(8,128)(2,1)S(1)}, bf16[96,512]{1,0:T(8,128)(2,1)S(1)}, u32[]{:S(2)}, u32[]{:S(2)}) collective-permute-start(bf16[96,512]{1,0:T(8,128)(2,1)S(1)} %smear.1.rest_0_), channel_id=1, source_target_pairs={{0,2},{2,0},{4,6},{6,4},{8,10},{10,8},{12,14},{14,12},{1,3},{3,1},... | collective-permute-start | bytes 294920 | tf_op jit(solution)/shard_map/ppermute | solution.py:322
  38.3 1.1 %collective-permute-done.6.rest_3_ = bf16[96,512]{1,0:T(8,128)(2,1)S(1)} collective-permute-done((bf16[96,512]{1,0:T(8,128)(2,1)S(1)}, bf16[96,512]{1,0:T(8,128)(2,1)S(1)}, u32[]{:S(2)}, u32[]{:S(2)}) %collective-permute-start.6) | collective-permute-done | bytes 98336 | tf_op jit(solution)/shard_map/ppermute | solution.py:326
  39.4 1.5 %collective-permute-start.10 = (bf16[96,512]{1,0:T(8,128)(2,1)S(1)}, bf16[96,512]{1,0:T(8,128)(2,1)S(1)}, u32[]{:S(2)}, u32[]{:S(2)}) collective-permute-start(bf16[96,512]{1,0:T(8,128)(2,1)S(1)} %collective-permute-done.6.rest_3_), channel_id=1, source_target_pairs={{0,2},{2,0},{4,6},{6,4},{8,10},{10,8},{12,14},{14,12},{1,3},{3,1},... | collective-permute-start | bytes 294920 | tf_op jit(solution)/shard_map/ppermute | solution.py:322
  40.9 4.7 %collective-permute-done.5.rest_2_ = bf16[96,512]{1,0:T(8,128)(2,1)S(1)} collective-permute-done((bf16[96,512]{1,0:T(8,128)(2,1)S(1)}, bf16[96,512]{1,0:T(8,128)(2,1)S(1)}, u32[]{:S(2)}, u32[]{:S(2)}) %collective-permute-start.5) | collective-permute-done | bytes 98336 | tf_op jit(solution)/shard_map/ppermute | solution.py:326
  45.6 1.5 %collective-permute-start.9 = (bf16[96,512]{1,0:T(8,128)(2,1)S(1)}, bf16[96,512]{1,0:T(8,128)(2,1)S(1)}, u32[]{:S(2)}, u32[]{:S(2)}) collective-permute-start(bf16[96,512]{1,0:T(8,128)(2,1)S(1)} %collective-permute-done.5.rest_2_), channel_id=1, source_target_pairs={{0,2},{2,0},{4,6},{6,4},{8,10},{10,8},{12,14},{14,12},{1,3},{3,1},... | collective-permute-start | bytes 294920 | tf_op jit(solution)/shard_map/ppermute | solution.py:322
  47.1 0.0 collective-permute-done.4.rest_1_
  47.1 0.6 collective-permute-start.8
  47.6 0.0 collective-permute-done.7.rest_4_
  47.6 0.0 collective-permute-done.10.rest_7_
  47.6 3.0 %collective-permute-done.9.rest_6_ = bf16[96,512]{1,0:T(8,128)(2,1)S(1)} collective-permute-done((bf16[96,512]{1,0:T(8,128)(2,1)S(1)}, bf16[96,512]{1,0:T(8,128)(2,1)S(1)}, u32[]{:S(2)}, u32[]{:S(2)}) %collective-permute-start.9) | collective-permute-done | bytes 98336 | tf_op jit(solution)/shard_map/ppermute | solution.py:322
  50.7 1.1 %collective-permute-done.8.rest_5_ = bf16[96,512]{1,0:T(8,128)(2,1)S(1)} collective-permute-done((bf16[96,512]{1,0:T(8,128)(2,1)S(1)}, bf16[96,512]{1,0:T(8,128)(2,1)S(1)}, u32[]{:S(2)}, u32[]{:S(2)}) %collective-permute-start.8) | collective-permute-done | bytes 98336 | tf_op jit(solution)/shard_map/ppermute | solution.py:322
  51.7 0.0 copy-start
  51.7 1.9 %copy-done = bf16[1,16,2,3,8,2048]{5,4,3,2,1,0:T(8,128)(2,1)S(1)} copy-done((bf16[1,16,2,3,8,2048]{5,4,3,2,1,0:T(8,128)(2,1)S(1)}, bf16[1,16,2,3,8,2048]{5,4,3,2,1,0:T(8,128)(2,1)}, u32[]{:S(2)}) %copy-start) | copy-done | bytes 3145752
  53.6 0.0 copy-start.3
  53.6 0.9 %copy-done.3 = f32[104,192]{1,0:T(8,128)S(1)} copy-done((f32[104,192]{1,0:T(8,128)S(1)}, f32[104,192]{1,0:T(8,128)}, u32[]{:S(2)}) %copy-start.3) | copy-done | bytes 79896
  54.5 1.9 %project.1 = (bf16[24,2048]{1,0:T(8,128)(2,1)S(1)}, f32[16,8]{1,0:T(8,128)S(1)}) custom-call(s32[2]{0:T(128)S(1)} %pad_add_fusion.place, bf16[768,2048]{1,0:T(8,128)(2,1)S(1)} %bitcast.7, f32[104,192]{1,0:T(8,128)S(1)} %copy-done.3, bf16[96,512]{1,0:T(8,128)(2,1)S(1)} %smear.1.rest_0_, bf16[96,512]{1,0:T(8,128)(2,1)S(1)} %collective-permute-done.4.rest_1_, ...), custom_call_target="tpu_custom_call" | custom-call | tf_op jit(solution)/shard_map/project/pallas_call | solution.py:365
  56.4 0.7 %copy.9 = f32[16,8]{0,1:T(8,128)} copy(f32[16,8]{1,0:T(8,128)S(1)} %get-tuple-element.13) | data formatting | bytes 1024 | tf_op jit(solution)/shard_map/project/pallas_call | solution.py:365
  57.0 0.1 reshape.22
  57.1 0.8 %copy.10 = bf16[1,4,2,3,1,2048]{5,2,4,3,1,0:T(2,128)(2,1)} copy(bf16[1,4,2,3,1,2048]{5,3,2,1,4,0:T(4,128)(2,1)S(1)} %reshape.22) | data formatting | bytes 196608
Async XLA Ops:
  2.9 5.4 %collective-permute-start = (bf16[312,128]{1,0:T(8,128)(2,1)S(1)}, bf16[312,128]{1,0:T(8,128)(2,1)S(1)}, u32[]{:S(2)}, u32[]{:S(2)}) collective-permute-start(bf16[312,128]{1,0:T(8,128)(2,1)S(1)} %bitcast.12), channel_id=1, source_target_pairs={{0,2},{2,0},{4,6},{6,4},{8,10},{10,8},{12,14},{14,12},{1,3},{3,1},... | collective-permute-start | bytes 239624 | tf_op jit(solution)/shard_map/ppermute | solution.py:322
  8.3 1.0 %copy-start.1 = (f32[1,3,2,3,3,1,2048]{6,5,4,3,2,1,0:T(1,128)S(1)}, f32[1,3,2,3,3,1,2048]{6,5,4,3,2,1,0:T(1,128)}, u32[]{:S(2)}) copy-start(f32[1,3,2,3,3,1,2048]{6,5,4,3,2,1,0:T(1,128)} %param.6) | copy-start | bytes 1327108
  9.3 0.9 %copy-start.2 = (f32[1,4,2,3,1,2048]{5,4,3,2,1,0:T(1,128)S(1)}, f32[1,4,2,3,1,2048]{5,4,3,2,1,0:T(1,128)}, u32[]{:S(2)}) copy-start(f32[1,4,2,3,1,2048]{5,4,3,2,1,0:T(1,128)} %param.5) | copy-start | bytes 589828
  11.0 9.3 %collective-permute-start.1 = (bf16[624,128]{1,0:T(8,128)(2,1)S(1)}, bf16[624,128]{1,0:T(8,128)(2,1)S(1)}, u32[]{:S(2)}, u32[]{:S(2)}) collective-permute-start(bf16[624,128]{1,0:T(8,128)(2,1)S(1)} %get-tuple-element.9), channel_id=1, source_target_pairs={{0,4},{2,6},{4,8},{6,10},{8,12},{10,14},{12,0},{14,2},{1,5},{3,7},... | collective-permute-start | bytes 479240 | tf_op jit(solution)/shard_map/ppermute | solution.py:326
  13.1 11.9 %collective-permute-start.2 = (bf16[624,128]{1,0:T(8,128)(2,1)S(1)}, bf16[624,128]{1,0:T(8,128)(2,1)S(1)}, u32[]{:S(2)}, u32[]{:S(2)}) collective-permute-start(bf16[624,128]{1,0:T(8,128)(2,1)S(1)} %get-tuple-element.10), channel_id=1, source_target_pairs={{0,8},{2,10},{4,12},{6,14},{8,0},{10,2},{12,4},{14,6},{1,9},{3,11}... | collective-permute-start | bytes 479240 | tf_op jit(solution)/shard_map/ppermute | solution.py:326
  15.7 9.3 %collective-permute-start.3 = (bf16[624,128]{1,0:T(8,128)(2,1)S(1)}, bf16[624,128]{1,0:T(8,128)(2,1)S(1)}, u32[]{:S(2)}, u32[]{:S(2)}) collective-permute-start(bf16[624,128]{1,0:T(8,128)(2,1)S(1)} %get-tuple-element.11), channel_id=1, source_target_pairs={{0,12},{2,14},{4,0},{6,2},{8,4},{10,6},{12,8},{14,10},{1,13},{3,15... | collective-permute-start | bytes 479240 | tf_op jit(solution)/shard_map/ppermute | solution.py:326
  31.2 8.2 %collective-permute-start.6 = (bf16[96,512]{1,0:T(8,128)(2,1)S(1)}, bf16[96,512]{1,0:T(8,128)(2,1)S(1)}, u32[]{:S(2)}, u32[]{:S(2)}) collective-permute-start(bf16[96,512]{1,0:T(8,128)(2,1)S(1)} %smear.1.rest_0_), channel_id=1, source_target_pairs={{0,12},{2,14},{4,0},{6,2},{8,4},{10,6},{12,8},{14,10},{1,13},{3,15... | collective-permute-start | bytes 294920 | tf_op jit(solution)/shard_map/ppermute | solution.py:326
  36.2 9.4 %collective-permute-start.5 = (bf16[96,512]{1,0:T(8,128)(2,1)S(1)}, bf16[96,512]{1,0:T(8,128)(2,1)S(1)}, u32[]{:S(2)}, u32[]{:S(2)}) collective-permute-start(bf16[96,512]{1,0:T(8,128)(2,1)S(1)} %smear.1.rest_0_), channel_id=1, source_target_pairs={{0,8},{2,10},{4,12},{6,14},{8,0},{10,2},{12,4},{14,6},{1,9},{3,11}... | collective-permute-start | bytes 294920 | tf_op jit(solution)/shard_map/ppermute | solution.py:326
  36.6 10.5 %collective-permute-start.4 = (bf16[96,512]{1,0:T(8,128)(2,1)S(1)}, bf16[96,512]{1,0:T(8,128)(2,1)S(1)}, u32[]{:S(2)}, u32[]{:S(2)}) collective-permute-start(bf16[96,512]{1,0:T(8,128)(2,1)S(1)} %smear.1.rest_0_), channel_id=1, source_target_pairs={{0,4},{2,6},{4,8},{6,10},{8,12},{10,14},{12,0},{14,2},{1,5},{3,7},... | collective-permute-start | bytes 294920 | tf_op jit(solution)/shard_map/ppermute | solution.py:326
  36.8 10.8 %collective-permute-start.7 = (bf16[96,512]{1,0:T(8,128)(2,1)S(1)}, bf16[96,512]{1,0:T(8,128)(2,1)S(1)}, u32[]{:S(2)}, u32[]{:S(2)}) collective-permute-start(bf16[96,512]{1,0:T(8,128)(2,1)S(1)} %smear.1.rest_0_), channel_id=1, source_target_pairs={{0,2},{2,0},{4,6},{6,4},{8,10},{10,8},{12,14},{14,12},{1,3},{3,1},... | collective-permute-start | bytes 294920 | tf_op jit(solution)/shard_map/ppermute | solution.py:322
  39.4 8.3 %collective-permute-start.10 = (bf16[96,512]{1,0:T(8,128)(2,1)S(1)}, bf16[96,512]{1,0:T(8,128)(2,1)S(1)}, u32[]{:S(2)}, u32[]{:S(2)}) collective-permute-start(bf16[96,512]{1,0:T(8,128)(2,1)S(1)} %collective-permute-done.6.rest_3_), channel_id=1, source_target_pairs={{0,2},{2,0},{4,6},{6,4},{8,10},{10,8},{12,14},{14,12},{1,3},{3,1},... | collective-permute-start | bytes 294920 | tf_op jit(solution)/shard_map/ppermute | solution.py:322
  45.6 5.1 %collective-permute-start.9 = (bf16[96,512]{1,0:T(8,128)(2,1)S(1)}, bf16[96,512]{1,0:T(8,128)(2,1)S(1)}, u32[]{:S(2)}, u32[]{:S(2)}) collective-permute-start(bf16[96,512]{1,0:T(8,128)(2,1)S(1)} %collective-permute-done.5.rest_2_), channel_id=1, source_target_pairs={{0,2},{2,0},{4,6},{6,4},{8,10},{10,8},{12,14},{14,12},{1,3},{3,1},... | collective-permute-start | bytes 294920 | tf_op jit(solution)/shard_map/ppermute | solution.py:322
  47.1 4.6 %collective-permute-start.8 = (bf16[96,512]{1,0:T(8,128)(2,1)S(1)}, bf16[96,512]{1,0:T(8,128)(2,1)S(1)}, u32[]{:S(2)}, u32[]{:S(2)}) collective-permute-start(bf16[96,512]{1,0:T(8,128)(2,1)S(1)} %collective-permute-done.4.rest_1_), channel_id=1, source_target_pairs={{0,2},{2,0},{4,6},{6,4},{8,10},{10,8},{12,14},{14,12},{1,3},{3,1},... | collective-permute-start | bytes 294920 | tf_op jit(solution)/shard_map/ppermute | solution.py:322
  51.7 1.9 %copy-start = (bf16[1,16,2,3,8,2048]{5,4,3,2,1,0:T(8,128)(2,1)S(1)}, bf16[1,16,2,3,8,2048]{5,4,3,2,1,0:T(8,128)(2,1)}, u32[]{:S(2)}) copy-start(bf16[1,16,2,3,8,2048]{5,4,3,2,1,0:T(8,128)(2,1)} %param.7) | copy-start | bytes 9437188
  53.6 0.9 %copy-start.3 = (f32[104,192]{1,0:T(8,128)S(1)}, f32[104,192]{1,0:T(8,128)}, u32[]{:S(2)}) copy-start(f32[104,192]{1,0:T(8,128)} %constant.35.clone.masks) | copy-start | bytes 239620

commit v2 on v0

--- a/solution.py
+++ b/solution.py
@@ -1,6 +1,8 @@
 import jax
 import jax.numpy as jnp
 from jax import lax
+from jax.experimental import pallas as pl
+from jax.experimental.pallas import tpu as pltpu
 from jax.sharding import PartitionSpec as P
 
 NSMEAR = 4
@@ -114,7 +116,7 @@
     return jnp.einsum("tkm,tvm->tkv", left_flat, right_flat, preferred_element_type=jnp.float32)
 
 
-def local(solutions, links, eigvecs):
+def by_planes(solutions, links, eigvecs):
     slices = solutions.shape[0]
     vectors = solutions.shape[1]
     real = solutions[:, :, 0].reshape(slices, vectors, 3, -1)
@@ -129,6 +131,362 @@
     return (smeared, coefficients)
 
 
+PLANES = 4
+FIELDS = 24
+LINKS = 54
+PARTS = FIELDS + LINKS
+WINDOW = PARTS * 8
+
+
+def is_diagonal(part):
+    return part >= FIELDS and (part - FIELDS) % 18 in (0, 4, 8)
+
+
+def my_place():
+    me = lax.axis_index("space")
+    return me // 2, lax.rem(me, 2)
+
+
+def slab_of(z, h):
+    return jnp.where(h == 0, z, PLANES - 1 - z)
+
+
+def read_kernel(field, link, ends, wide, narrow, field_done, link_done):
+    field_copy = pltpu.make_async_copy(field, wide.at[:FIELDS], field_done)
+    link_copy = pltpu.make_async_copy(link, wide.at[FIELDS:], link_done)
+    field_copy.start()
+    link_copy.start()
+    field_copy.wait()
+    link_copy.wait()
+    for part in range(PARTS):
+        if is_diagonal(part):
+            wide[part] = wide[part] - 1.0
+        narrow[4 * part : 4 * part + 2, :] = wide[part, 0:2, :]
+        narrow[4 * part + 2 : 4 * part + 4, :] = wide[part, 14:16, :]
+    ends[...] = narrow[...].astype(jnp.bfloat16)
+
+
+def pack_kernel(wide, ends, *rest):
+    outs, window, windows, narrow = rest[:PLANES], *rest[PLANES:]
+    z, h = my_place()
+    narrow[...] = ends[...].astype(jnp.float32)
+    for slab in range(PLANES):
+        low, high = max(4 * slab - 2, 0), min(4 * slab + 6, 16)
+        to = low - (4 * slab - 2)
+        window[:, to : to + high - low, :] = wide[:, low:high, :]
+        for part in range(PARTS):
+            if slab == 0:
+                window[part, 0:2, :] = narrow[4 * part + 2 : 4 * part + 4, :]
+            if slab == PLANES - 1:
+                window[part, 6:8, :] = narrow[4 * part : 4 * part + 2, :]
+        windows[slab] = window[...].reshape(WINDOW, 128).astype(jnp.bfloat16)
+    for hop in range(PLANES):
+        outs[hop][...] = windows[slab_of(lax.rem(z + hop, PLANES), h)]
+
+
+def by_color(part):
+    vector, rest = part // 6, part % 6
+    return vector * 6 + rest % 3 * 2 + rest // 3
+
+
+def apply_links(entry, sign, field):
+    reals = []
+    imags = []
+    for row in range(3):
+        real = imag = None
+        for inner in range(3):
+            re, im = entry(row, inner)
+            real_a, real_b = re * field[inner], im * field[3 + inner]
+            imag_a, imag_b = re * field[3 + inner], im * field[inner]
+            if sign > 0:
+                term_real, term_imag = real_a - real_b, imag_a + imag_b
+            else:
+                term_real, term_imag = real_a + real_b, imag_a - imag_b
+            real = term_real if real is None else real + term_real
+            imag = term_imag if imag is None else imag + term_imag
+        reals.append(real)
+        imags.append(imag)
+    return reals + imags
+
+
+def smear_kernel(*rest):
+    blocks, (out, phi, links, flat) = rest[:PLANES], rest[PLANES:]
+    lane = lax.broadcasted_iota(jnp.int32, (8, 128), 1)
+    x_place = lane % LX
+    at_end = x_place == LX - 1
+    at_start = x_place == 0
+    low = lane < LX
+
+    def scaled(part, value):
+        return kappa_hop * (value + 1.0 if is_diagonal(part) else value)
+
+    for plane in range(PLANES):
+        values = blocks[plane][...].astype(jnp.float32).reshape(PARTS, 8, 128)
+        for part in range(FIELDS):
+            phi[0, plane, by_color(part)] = values[part]
+        for part in range(FIELDS, PARTS):
+            links[plane, part - FIELDS] = scaled(part, values[part])
+
+    def next_x(a):
+        return jnp.where(at_end, pltpu.roll(a, LX - 1, 1), pltpu.roll(a, 127, 1))
+
+    def last_x(a):
+        return jnp.where(at_start, pltpu.roll(a, LX + 1, 1), pltpu.roll(a, 1, 1))
+
+    def next_y(a):
+        other = pltpu.roll(a, LX, 1)
+        return jnp.where(low, other, pltpu.roll(other, 7, 0))
+
+    def last_y(a):
+        other = pltpu.roll(a, LX, 1)
+        return jnp.where(low, pltpu.roll(other, 1, 0), other)
+
+    def forward(plane, along, field):
+        def entry(row, inner):
+            at = along * 18 + row * 3 + inner
+            return links[plane, at], links[plane, at + 9]
+
+        return apply_links(entry, 1, field)
+
+    def backward(plane, along, field):
+        def entry(row, inner):
+            at = along * 18 + inner * 3 + row
+            return links[plane, at], links[plane, at + 9]
+
+        return apply_links(entry, -1, field)
+
+    def one_step(source, target):
+        def one(plane, carry):
+            above = lax.rem(plane + 3, PLANES)
+            below = lax.rem(plane + 1, PLANES)
+            for vector in range(FIELDS // 6):
+                base = vector * 6
+                field = [phi[source, plane, base + by_color(i)] for i in range(6)]
+                upper = [phi[source, above, base + by_color(i)] for i in range(6)]
+                lower = [phi[source, below, base + by_color(i)] for i in range(6)]
+                total = [(1.0 - 6.0 * kappa_hop) * a for a in field]
+                for terms in (
+                    [last_x(a) for a in backward(plane, 0, field)],
+                    [last_y(a) for a in backward(plane, 1, field)],
+                    forward(plane, 2, upper),
+                    backward(below, 2, lower),
+                    forward(plane, 0, [next_x(a) for a in field]),
+                    forward(plane, 1, [next_y(a) for a in field]),
+                ):
+                    total = [a + b for a, b in zip(total, terms)]
+                for i in range(6):
+                    phi[target, plane, base + by_color(i)] = total[i]
+            return carry
+
+        lax.fori_loop(0, PLANES, one, 0)
+
+    for step in range(NSMEAR):
+        one_step(step % 2, (step + 1) % 2)
+
+    last = NSMEAR % 2
+    for plane in range(PLANES):
+        true_plane = lax.rem(my_place()[0] + PLANES - plane, PLANES)
+        for row in range(4):
+            flat[true_plane, :, row * 128 : (row + 1) * 128] = phi[last, plane, :, 2 + row, :]
+    out[...] = flat[...].reshape(PLANES * FIELDS, 512).astype(jnp.bfloat16)
+
+
+def column_start(z, hop, side):
+    slab = slab_of(lax.rem(z + PLANES - hop, PLANES), side)
+    return pl.ds(pl.multiple_of(slab * 512, 512), 512)
+
+
+def own_plane_kernel(*rest):
+    blocks, out, column = rest[:PLANES], rest[PLANES], rest[PLANES + 1]
+    z, h = my_place()
+    for hop in range(PLANES):
+        block = blocks[hop][...].astype(jnp.float32).reshape(PLANES, FIELDS, 512)
+        column[:, :, column_start(z, hop, h)] = block
+    out[...] = column[z].reshape(out.shape).astype(jnp.bfloat16)
+
+
+FAR = 2
+
+
+def reduce_sites(eigvecs, columns, sites, masks, vectors, sums):
+    count = 4
+    width = sites.shape[0]
+    for group in range(eigvecs.shape[0] // (48 * count)):
+        rows = eigvecs[group * 48 * count : (group + 1) * 48 * count, columns]
+        product = lax.dot_general(
+            rows, sites[...], (((1,), (1,)), ((), ())), preferred_element_type=jnp.float32
+        ).reshape(count, 48, width)
+        for part in range(2):
+            sums[part, group * count : (group + 1) * count, :] = jnp.sum(
+                product * masks[part][None], axis=1
+            )
+    return [
+        lax.dot_general(
+            vectors,
+            sums[part],
+            (((1,), (1,)), ((), ())),
+            precision=lax.Precision.HIGHEST,
+            preferred_element_type=jnp.float32,
+        )[:4]
+        for part in range(2)
+    ]
+
+
+def project_near_kernel(eigvecs, *rest):
+    own, other = rest[:PLANES], list(rest[PLANES : 2 * PLANES - 1])
+    coefficients, sites, sums = rest[2 * PLANES - 1 :]
+    other.insert(FAR, None)
+    half = PLANES * FIELDS
+    z, h = my_place()
+    for hop in range(PLANES):
+        for blocks, side in ((own, h), (other, 1 - h)):
+            rows = pl.ds(pl.multiple_of(side * half, half), half)
+            here = jnp.zeros((half, 512), jnp.bfloat16) if blocks[hop] is None else blocks[hop][...]
+            sites[rows, column_start(z, hop, side)] = here
+    masks, vectors = projection_masks(2 * half, 0)
+    parts = reduce_sites(eigvecs, slice(None), sites, masks, vectors, sums)
+    for part in range(2):
+        coefficients[4 * part : 4 * part + 4, :] = parts[part]
+
+
+def project_far_kernel(eigvecs, near, block, coefficients, sums):
+    z, h = my_place()
+    masks, vectors = projection_masks(PLANES * FIELDS, 1 - h)
+    parts = reduce_sites(eigvecs, column_start(z, FAR, 1 - h), block, masks, vectors, sums)
+    for part in range(2):
+        rows = slice(4 * part, 4 * part + 4)
+        coefficients[rows, :] = near[rows, :] + parts[part]
+
+
+def divided(a, by):
+    return lax.shift_right_logical(a * (65536 // by + 1), 16)
+
+
+def projection_masks(width, side):
+    shape = (48, width)
+    row = lax.broadcasted_iota(jnp.int32, shape, 0)
+    column = lax.broadcasted_iota(jnp.int32, shape, 1)
+    ri = lax.shift_right_logical(row + 8, 5)
+    color = lax.shift_right_logical(row, 3) - 3 * ri
+    pair = lax.shift_right_logical(column, 1)
+    ri_right = column - 2 * pair
+    vector = divided(pair, 3)
+    color_right = pair - 3 * vector
+    site_row = divided(column, FIELDS)
+    site_row = 2 * (site_row & 3) + lax.shift_right_logical(site_row, 2) + side
+    here = (color == color_right) & ((row & 7) == site_row)
+    real = jnp.where(here & (ri == ri_right), 1.0, 0.0)
+    imag = jnp.where(here & (ri != ri_right), jnp.where(ri == 0, 1.0, -1.0), 0.0)
+    vectors = jnp.where((vector & 3)[:8] == lax.broadcasted_iota(jnp.int32, (8, shape[1]), 0), 1.0, 0.0)
+    return (real, imag), vectors
+
+
+def in_vmem(count):
+    return [pl.BlockSpec(memory_space=pltpu.VMEM)] * count
+
+
+def in_slabs(solutions, links, eigvecs):
+    in_hbm = [pl.BlockSpec(memory_space=pltpu.HBM)]
+    limit = pltpu.CompilerParams(vmem_limit_bytes=8 * 1024 * 1024)
+    count = 2 * PLANES
+
+    def swapped(block):
+        return lax.ppermute(block, "space", [(i, i ^ 1) for i in range(count)])
+
+    def moved_up(block, planes):
+        return lax.ppermute(block, "space", [(i, (i + 2 * planes) % count) for i in range(count)])
+
+    ends, wide = pl.pallas_call(
+        read_kernel,
+        out_shape=[
+            jax.ShapeDtypeStruct((4 * PARTS, 128), jnp.bfloat16),
+            jax.ShapeDtypeStruct((PARTS, 16, 128), jnp.float32),
+        ],
+        in_specs=in_hbm * 2,
+        out_specs=in_vmem(2),
+        scratch_shapes=[
+            pltpu.VMEM((4 * PARTS, 128), jnp.float32),
+            pltpu.SemaphoreType.DMA(()),
+            pltpu.SemaphoreType.DMA(()),
+        ],
+        compiler_params=pltpu.CompilerParams(vmem_limit_bytes=63 * 1024 * 1024),
+        name="read",
+    )(solutions.reshape(FIELDS, 16, 128), links.reshape(LINKS, 16, 128))
+    packed = pl.pallas_call(
+        pack_kernel,
+        out_shape=[jax.ShapeDtypeStruct((WINDOW, 128), jnp.bfloat16)] * PLANES,
+        in_specs=in_vmem(2),
+        out_specs=in_vmem(PLANES),
+        scratch_shapes=[
+            pltpu.VMEM((PARTS, 8, 128), jnp.float32),
+            pltpu.VMEM((PLANES, WINDOW, 128), jnp.bfloat16),
+            pltpu.VMEM((4 * PARTS, 128), jnp.float32),
+        ],
+        compiler_params=limit,
+        name="pack",
+    )(wide, swapped(ends))
+    vectors = eigvecs.shape[1]
+    blocks = [packed[0]] + [moved_up(packed[hop], hop) for hop in range(1, PLANES)]
+    vectors = eigvecs.shape[1]
+    block = pl.pallas_call(
+        smear_kernel,
+        out_shape=jax.ShapeDtypeStruct((PLANES * FIELDS, 512), jnp.bfloat16),
+        in_specs=in_vmem(PLANES),
+        out_specs=pl.BlockSpec(memory_space=pltpu.VMEM),
+        scratch_shapes=[
+            pltpu.VMEM((2, PLANES, FIELDS, 8, 128), jnp.float32),
+            pltpu.VMEM((PLANES, LINKS, 8, 128), jnp.float32),
+            pltpu.VMEM((PLANES, FIELDS, 512), jnp.float32),
+        ],
+        compiler_params=limit,
+        cost_estimate=pl.CostEstimate(flops=10**9, bytes_accessed=2 * 10**7, transcendentals=0),
+        name="smear",
+    )(*blocks)
+    own = [block] + [moved_up(block, hop) for hop in range(1, PLANES)]
+    own[FAR] = lax.optimization_barrier((own[FAR], own[1], own[3]))[0]
+    other = [swapped(part) for part in own]
+    smeared = pl.pallas_call(
+        own_plane_kernel,
+        out_shape=jax.ShapeDtypeStruct((FIELDS // 2, 2, 2048), jnp.bfloat16),
+        in_specs=in_vmem(PLANES),
+        out_specs=pl.BlockSpec(memory_space=pltpu.VMEM),
+        scratch_shapes=[pltpu.VMEM((PLANES, FIELDS, 2048), jnp.float32)],
+        compiler_params=limit,
+        name="own_plane",
+    )(*own)
+    eigvecs = eigvecs.reshape(vectors * 48, 2048)
+    near = pl.pallas_call(
+        project_near_kernel,
+        out_shape=jax.ShapeDtypeStruct((8, vectors), jnp.float32),
+        in_specs=in_vmem(2 * PLANES),
+        out_specs=pl.BlockSpec(memory_space=pltpu.VMEM),
+        scratch_shapes=[
+            pltpu.VMEM((2 * PLANES * FIELDS, 2048), jnp.bfloat16),
+            pltpu.VMEM((2, vectors, 2 * PLANES * FIELDS), jnp.float32),
+        ],
+        compiler_params=limit,
+        cost_estimate=pl.CostEstimate(flops=10**9, bytes_accessed=4 * 10**6, transcendentals=0),
+        name="project_near",
+    )(eigvecs, *own, *other[:FAR], *other[FAR + 1 :])
+    coefficients = pl.pallas_call(
+        project_far_kernel,
+        out_shape=jax.ShapeDtypeStruct((8, vectors), jnp.float32),
+        in_specs=in_vmem(3),
+        out_specs=pl.BlockSpec(memory_space=pltpu.VMEM),
+        scratch_shapes=[pltpu.VMEM((2, vectors, PLANES * FIELDS), jnp.float32)],
+        compiler_params=limit,
+        name="project_far",
+    )(eigvecs, near, other[FAR])
+    smeared = smeared.reshape(1, 4, 3, 2, 1, 2048).swapaxes(2, 3)
+    return smeared, coefficients.T[None]
+
+
+def local(solutions, links, eigvecs):
+    fits = lax.axis_size("space") == 2 * PLANES and solutions.shape[:2] == (1, 4)
+    fits = fits and solutions.shape[4:] == (1, 2048) and eigvecs.shape[1] % 4 == 0
+    return (in_slabs if fits else by_planes)(solutions, links, eigvecs)
+
+
 def solution(mesh):
     placed = (
         P(("cfg", "tm"), None, None, None, "space", None),

time: 97.5 us -> 48.8 us (0.50)
  blocking collectives: 32.5 us -> 0 us
  other arithmetic: 17.3 us -> 0 us
  Pallas kernels: 0 us -> 10.3 us
  local copies, waits for them, and re-layouts: 9.41 us -> 1.09 us
  waiting for transfers between devices: 8.32 us -> 15.9 us
  matrix products: 4.62 us -> 0 us
  starting transfers between devices: 23.2 us -> 20.7 us
  between operations: 1.87 us -> 0.68 us
    all_gather x1 -> x0, blocking collectives: 32.5 us -> none  [local(): lax.all_gather(smeared, 'space', axis=4, tiled=True)]
    pallas_call x0 -> x6, Pallas kernels: none -> 10.3 us  [the longest x1 4.79 us: in_slabs(): pl.pallas_call(smear_kernel, out_shape=jax.ShapeDtypeStruct((PLANES * FIE...]
    another operation x25 -> x0, other arithmetic: 10.1 us -> none
    ppermute x12 -> x11, waiting for transfers between devices: 8.32 us -> 15.9 us  [the longest x6 12.3 us: moved_up(): lax.ppermute(block, 'space', [(i, (i + 2 * planes) % count) for i in rang...]
    dot_general x1 -> x0, matrix products: 4.62 us -> none  [project(): jnp.einsum('tkm,tvm->tkv', left_flat, right_flat, preferred_element_type=...]
    add x10 -> x0, other arithmetic: 4.31 us -> none  [the longest x3 1.59 us: local(): imag = imag + kappa_hop * (hop_imag - 6.0 * imag)]
    slice x40 -> x0, local copies, waits for them, and re-layouts: 3.59 us -> none  [the longest x1 1.11 us: local(): real = solutions[:, :, 0].reshape(slices, vectors, 3, -1)]
    ppermute x12 -> x11, starting transfers between devices: 23.2 us -> 20.7 us  [the longest x6 11.7 us: moved_up(): lax.ppermute(block, 'space', [(i, (i + 2 * planes) % count) for i in rang...]
  transfers between devices with their start and end apart: 12 -> 11, of which waited for: 5 -> 7; matrix products, arithmetic and copies ran while one was open for 10% -> 0% of each run, Pallas kernels for 0% -> 4%
where the time goes in v2:
time: 48.8 us; the launch traced here: 48.6 us
  starting transfers between devices  20.7 us (42%)
  waiting for transfers between devices  15.9 us (33%)
  Pallas kernels  10.3 us (21%)
  local copies, waits for them, and re-layouts  1.09 us (2%)
  between operations  0.68 us (1%)
    ppermute x6, waiting for transfers between devices, moved_up(): lax.ppermute(block, 'space', [(i, (i + 2 * planes) % count) for i in rang...  12.3 us
    ppermute x6, starting transfers between devices, moved_up(): lax.ppermute(block, 'space', [(i, (i + 2 * planes) % count) for i in rang...  11.7 us
    ppermute x5, starting transfers between devices, swapped(): return lax.ppermute(block, 'space', [(i, i ^ 1) for i in range(count)])  8.97 us
    pallas_call x1, Pallas kernels, in_slabs(): pl.pallas_call(smear_kernel, out_shape=jax.ShapeDtypeStruct((PLANES * FIE...  4.79 us
    ppermute x5, waiting for transfers between devices, swapped(): return lax.ppermute(block, 'space', [(i, i ^ 1) for i in range(count)])  3.58 us
    pallas_call x1, Pallas kernels, in_slabs(): pl.pallas_call(read_kernel, out_shape=[jax.ShapeDtypeStruct((4 * PARTS, 1...  2.02 us
    pallas_call x1, Pallas kernels, in_slabs(): pl.pallas_call(project_near_kernel, out_shape=jax.ShapeDtypeStruct((8, ve...  1.34 us
    pallas_call x1, Pallas kernels, in_slabs(): pl.pallas_call(project_far_kernel, out_shape=jax.ShapeDtypeStruct((8, vec...  1.11 us
  transfers between devices with their start and end apart: 11, of which 7 were waited for; matrix products, arithmetic and copies ran while one was open for 0% of the time, Pallas kernels for 4%

profile of v2, /device:TPU:0, one launch (start us, length us, event | category | flops | bytes accessed | tf_op | source)
XLA Modules:
  0.0 48.6 jit_solution(371155302589519997)
XLA Ops:
  0.6 2.0 %read.1 = (bf16[312,128]{1,0:T(8,128)(2,1)}, f32[78,16,128]{2,1,0:T(8,128)}) custom-call(f32[24,16,128]{2,1,0:T(8,128)} %bitcast.14, f32[54,16,128]{2,1,0:T(8,128)} %bitcast.13), custom_call_target="tpu_custom_call" | custom-call | tf_op jit(solution)/shard_map/read/pallas_call | solution.py:399
  2.7 0.0 copy-start
  2.7 3.0 %collective-permute-start = (bf16[312,128]{1,0:T(8,128)(2,1)}, bf16[312,128]{1,0:T(8,128)(2,1)S(1)}, u32[]{:S(2)}, u32[]{:S(2)}) collective-permute-start(bf16[312,128]{1,0:T(8,128)(2,1)} %get-tuple-element.10), channel_id=1, source_target_pairs={{0,2},{2,0},{4,6},{6,4},{8,10},{10,8},{12,14},{14,12},{1,3},{3,1},... | collective-permute-start | bytes 239624 | tf_op jit(solution)/shard_map/ppermute | solution.py:394
  5.7 2.6 %collective-permute-done.ends = bf16[312,128]{1,0:T(8,128)(2,1)S(1)} collective-permute-done((bf16[312,128]{1,0:T(8,128)(2,1)}, bf16[312,128]{1,0:T(8,128)(2,1)S(1)}, u32[]{:S(2)}, u32[]{:S(2)}) %collective-permute-start) | collective-permute-done | bytes 79904 | tf_op jit(solution)/shard_map/ppermute | solution.py:394
  8.3 0.0 copy-start.1
  8.3 1.1 %copy-done.1 = f32[78,16,128]{2,1,0:T(8,128)S(1)} copy-done((f32[78,16,128]{2,1,0:T(8,128)S(1)}, f32[78,16,128]{2,1,0:T(8,128)}, u32[]{:S(2)}) %copy-start.1) | copy-done | bytes 639000
  9.4 0.2 pack.1
  9.6 2.2 %collective-permute-start.1 = (bf16[624,128]{1,0:T(8,128)(2,1)S(1)}, bf16[624,128]{1,0:T(8,128)(2,1)S(1)}, u32[]{:S(2)}, u32[]{:S(2)}) collective-permute-start(bf16[624,128]{1,0:T(8,128)(2,1)S(1)} %get-tuple-element.12), channel_id=1, source_target_pairs={{0,4},{2,6},{4,8},{6,10},{8,12},{10,14},{12,0},{14,2},{1,5},{3,7},... | collective-permute-start | bytes 479240 | tf_op jit(solution)/shard_map/ppermute | solution.py:397
  11.8 2.6 %collective-permute-start.2 = (bf16[624,128]{1,0:T(8,128)(2,1)S(1)}, bf16[624,128]{1,0:T(8,128)(2,1)S(1)}, u32[]{:S(2)}, u32[]{:S(2)}) collective-permute-start(bf16[624,128]{1,0:T(8,128)(2,1)S(1)} %get-tuple-element.13), channel_id=1, source_target_pairs={{0,8},{2,10},{4,12},{6,14},{8,0},{10,2},{12,4},{14,6},{1,9},{3,11}... | collective-permute-start | bytes 479240 | tf_op jit(solution)/shard_map/ppermute | solution.py:397
  14.3 1.3 %collective-permute-start.3 = (bf16[624,128]{1,0:T(8,128)(2,1)S(1)}, bf16[624,128]{1,0:T(8,128)(2,1)S(1)}, u32[]{:S(2)}, u32[]{:S(2)}) collective-permute-start(bf16[624,128]{1,0:T(8,128)(2,1)S(1)} %get-tuple-element.14), channel_id=1, source_target_pairs={{0,12},{2,14},{4,0},{6,2},{8,4},{10,6},{12,8},{14,10},{1,13},{3,15... | collective-permute-start | bytes 479240 | tf_op jit(solution)/shard_map/ppermute | solution.py:397
  15.7 3.2 %collective-permute-done.1.rest_1_ = bf16[624,128]{1,0:T(8,128)(2,1)S(1)} collective-permute-done((bf16[624,128]{1,0:T(8,128)(2,1)S(1)}, bf16[624,128]{1,0:T(8,128)(2,1)S(1)}, u32[]{:S(2)}, u32[]{:S(2)}) %collective-permute-start.1) | collective-permute-done | bytes 159776 | tf_op jit(solution)/shard_map/ppermute | solution.py:397
  18.9 4.8 %collective-permute-done.2.rest_2_ = bf16[624,128]{1,0:T(8,128)(2,1)S(1)} collective-permute-done((bf16[624,128]{1,0:T(8,128)(2,1)S(1)}, bf16[624,128]{1,0:T(8,128)(2,1)S(1)}, u32[]{:S(2)}, u32[]{:S(2)}) %collective-permute-start.2) | collective-permute-done | bytes 159776 | tf_op jit(solution)/shard_map/ppermute | solution.py:397
  23.7 0.0 collective-permute-done.3.rest_3_
  23.7 4.8 %smear.1.rest_0_ = bf16[96,512]{1,0:T(8,128)(2,1)S(1)} custom-call(bf16[624,128]{1,0:T(8,128)(2,1)S(1)} %get-tuple-element.11.rest_0_, bf16[624,128]{1,0:T(8,128)(2,1)S(1)} %collective-permute-done.1.rest_1_, bf16[624,128]{1,0:T(8,128)(2,1)S(1)} %collective-permute-done.2.rest_2_, bf16[624,128]{1,0:T(8,128)(2,1)S(1)} %collective-permute-done.3.rest_3_), custom_call_target="tpu_custom_call" | custom-call | flops 1000000000 | bytes 20000000 | tf_op jit(solution)/shard_map/smear/pallas_call | solution.py:431
  28.5 5.0 %collective-permute-start.6 = (bf16[96,512]{1,0:T(8,128)(2,1)S(1)}, bf16[96,512]{1,0:T(8,128)(2,1)S(1)}, u32[]{:S(2)}, u32[]{:S(2)}) collective-permute-start(bf16[96,512]{1,0:T(8,128)(2,1)S(1)} %smear.1.rest_0_), channel_id=1, source_target_pairs={{0,12},{2,14},{4,0},{6,2},{8,4},{10,6},{12,8},{14,10},{1,13},{3,15... | collective-permute-start | bytes 294920 | tf_op jit(solution)/shard_map/ppermute | solution.py:397
  33.5 0.0 collective-permute-start.4
  33.5 0.6 %collective-permute-start.5 = (bf16[96,512]{1,0:T(8,128)(2,1)S(1)}, bf16[96,512]{1,0:T(8,128)(2,1)S(1)}, u32[]{:S(2)}, u32[]{:S(2)}) collective-permute-start(bf16[96,512]{1,0:T(8,128)(2,1)S(1)} %smear.1.rest_0_), channel_id=1, source_target_pairs={{0,8},{2,10},{4,12},{6,14},{8,0},{10,2},{12,4},{14,6},{1,9},{3,11}... | collective-permute-start | bytes 294920 | tf_op jit(solution)/shard_map/ppermute | solution.py:397
  34.1 1.5 %collective-permute-start.7 = (bf16[96,512]{1,0:T(8,128)(2,1)S(1)}, bf16[96,512]{1,0:T(8,128)(2,1)S(1)}, u32[]{:S(2)}, u32[]{:S(2)}) collective-permute-start(bf16[96,512]{1,0:T(8,128)(2,1)S(1)} %smear.1.rest_0_), channel_id=1, source_target_pairs={{0,2},{2,0},{4,6},{6,4},{8,10},{10,8},{12,14},{14,12},{1,3},{3,1},... | collective-permute-start | bytes 294920 | tf_op jit(solution)/shard_map/ppermute | solution.py:394
  35.6 0.3 collective-permute-done.6.rest_3_
  35.9 1.5 %collective-permute-start.9 = (bf16[96,512]{1,0:T(8,128)(2,1)S(1)}, bf16[96,512]{1,0:T(8,128)(2,1)S(1)}, u32[]{:S(2)}, u32[]{:S(2)}) collective-permute-start(bf16[96,512]{1,0:T(8,128)(2,1)S(1)} %collective-permute-done.6.rest_3_), channel_id=1, source_target_pairs={{0,2},{2,0},{4,6},{6,4},{8,10},{10,8},{12,14},{14,12},{1,3},{3,1},... | collective-permute-start | bytes 294920 | tf_op jit(solution)/shard_map/ppermute | solution.py:394
  37.4 2.6 %collective-permute-done.4.rest_1_ = bf16[96,512]{1,0:T(8,128)(2,1)S(1)} collective-permute-done((bf16[96,512]{1,0:T(8,128)(2,1)S(1)}, bf16[96,512]{1,0:T(8,128)(2,1)S(1)}, u32[]{:S(2)}, u32[]{:S(2)}) %collective-permute-start.4) | collective-permute-done | bytes 98336 | tf_op jit(solution)/shard_map/ppermute | solution.py:397
  40.0 1.5 %collective-permute-start.8 = (bf16[96,512]{1,0:T(8,128)(2,1)S(1)}, bf16[96,512]{1,0:T(8,128)(2,1)S(1)}, u32[]{:S(2)}, u32[]{:S(2)}) collective-permute-start(bf16[96,512]{1,0:T(8,128)(2,1)S(1)} %collective-permute-done.4.rest_1_), channel_id=1, source_target_pairs={{0,2},{2,0},{4,6},{6,4},{8,10},{10,8},{12,14},{14,12},{1,3},{3,1},... | collective-permute-start | bytes 294920 | tf_op jit(solution)/shard_map/ppermute | solution.py:394
  41.5 1.4 %collective-permute-done.5.rest_2_ = bf16[96,512]{1,0:T(8,128)(2,1)S(1)} collective-permute-done((bf16[96,512]{1,0:T(8,128)(2,1)S(1)}, bf16[96,512]{1,0:T(8,128)(2,1)S(1)}, u32[]{:S(2)}, u32[]{:S(2)}) %collective-permute-start.5) | collective-permute-done | bytes 98336 | tf_op jit(solution)/shard_map/ppermute | solution.py:397
  42.9 1.5 %collective-permute-start.10 = (bf16[96,512]{1,0:T(8,128)(2,1)S(1)}, bf16[96,512]{1,0:T(8,128)(2,1)S(1)}, u32[]{:S(2)}, u32[]{:S(2)}) collective-permute-start(bf16[96,512]{1,0:T(8,128)(2,1)S(1)} %collective-permute-done.5.rest_2_), channel_id=1, source_target_pairs={{0,2},{2,0},{4,6},{6,4},{8,10},{10,8},{12,14},{14,12},{1,3},{3,1},... | collective-permute-start | bytes 294920 | tf_op jit(solution)/shard_map/ppermute | solution.py:394
  44.4 0.8 %own_plane.1 = bf16[12,2,2048]{2,1,0:T(2,128)(2,1)} custom-call(bf16[96,512]{1,0:T(8,128)(2,1)S(1)} %smear.1.rest_0_, bf16[96,512]{1,0:T(8,128)(2,1)S(1)} %collective-permute-done.4.rest_1_, bf16[96,512]{1,0:T(8,128)(2,1)S(1)} %collective-permute-done.5.rest_2_, bf16[96,512]{1,0:T(8,128)(2,1)S(1)} %collective-permute-done.6.rest_3_), custom_call_target="tpu_custom_call" | custom-call | tf_op jit(solution)/shard_map/own_plane/pallas_call | solution.py:448
  45.2 0.0 collective-permute-done.7.rest_4_
  45.2 0.0 collective-permute-done.9.rest_6_
  45.2 0.0 collective-permute-done.8.rest_5_
  45.2 0.0 copy-done
  45.2 1.3 %project_near.1.near = f32[8,16]{1,0:T(8,128)S(1)} custom-call(bf16[768,2048]{1,0:T(8,128)(2,1)S(1)} %bitcast.11, bf16[96,512]{1,0:T(8,128)(2,1)S(1)} %smear.1.rest_0_, bf16[96,512]{1,0:T(8,128)(2,1)S(1)} %collective-permute-done.4.rest_1_, bf16[96,512]{1,0:T(8,128)(2,1)S(1)} %collective-permute-done.5.rest_2_, ...), custom_call_target="tpu_custom_call" | custom-call | flops 1000000000 | bytes 4000000 | tf_op jit(solution)/shard_map/project_near/pallas_call | solution.py:458
  46.5 1.0 %collective-permute-done.10.block = bf16[96,512]{1,0:T(8,128)(2,1)S(1)} collective-permute-done((bf16[96,512]{1,0:T(8,128)(2,1)S(1)}, bf16[96,512]{1,0:T(8,128)(2,1)S(1)}, u32[]{:S(2)}, u32[]{:S(2)}) %collective-permute-start.10) | collective-permute-done | bytes 98336 | tf_op jit(solution)/shard_map/ppermute | solution.py:394
  47.5 1.1 %project_far.1 = f32[8,16]{1,0:T(8,128)} custom-call(bf16[768,2048]{1,0:T(8,128)(2,1)S(1)} %bitcast.12, f32[8,16]{1,0:T(8,128)S(1)} %project_near.1.near, bf16[96,512]{1,0:T(8,128)(2,1)S(1)} %collective-permute-done.10.block), custom_call_target="tpu_custom_call" | custom-call | tf_op jit(solution)/shard_map/project_far/pallas_call | solution.py:471
Async XLA Ops:
  2.7 42.6 %copy-start = (bf16[1,16,2,3,8,2048]{5,4,3,2,1,0:T(8,128)(2,1)S(1)}, bf16[1,16,2,3,8,2048]{5,4,3,2,1,0:T(8,128)(2,1)}, u32[]{:S(2)}) copy-start(bf16[1,16,2,3,8,2048]{5,4,3,2,1,0:T(8,128)(2,1)} %param.5) | copy-start | bytes 9437188
  2.7 5.6 %collective-permute-start = (bf16[312,128]{1,0:T(8,128)(2,1)}, bf16[312,128]{1,0:T(8,128)(2,1)S(1)}, u32[]{:S(2)}, u32[]{:S(2)}) collective-permute-start(bf16[312,128]{1,0:T(8,128)(2,1)} %get-tuple-element.10), channel_id=1, source_target_pairs={{0,2},{2,0},{4,6},{6,4},{8,10},{10,8},{12,14},{14,12},{1,3},{3,1},... | collective-permute-start | bytes 239624 | tf_op jit(solution)/shard_map/ppermute | solution.py:394
  8.3 1.1 %copy-start.1 = (f32[78,16,128]{2,1,0:T(8,128)S(1)}, f32[78,16,128]{2,1,0:T(8,128)}, u32[]{:S(2)}) copy-start(f32[78,16,128]{2,1,0:T(8,128)} %get-tuple-element.9.wide) | copy-start | bytes 1916932
  9.6 9.3 %collective-permute-start.1 = (bf16[624,128]{1,0:T(8,128)(2,1)S(1)}, bf16[624,128]{1,0:T(8,128)(2,1)S(1)}, u32[]{:S(2)}, u32[]{:S(2)}) collective-permute-start(bf16[624,128]{1,0:T(8,128)(2,1)S(1)} %get-tuple-element.12), channel_id=1, source_target_pairs={{0,4},{2,6},{4,8},{6,10},{8,12},{10,14},{12,0},{14,2},{1,5},{3,7},... | collective-permute-start | bytes 479240 | tf_op jit(solution)/shard_map/ppermute | solution.py:397
  11.8 11.9 %collective-permute-start.2 = (bf16[624,128]{1,0:T(8,128)(2,1)S(1)}, bf16[624,128]{1,0:T(8,128)(2,1)S(1)}, u32[]{:S(2)}, u32[]{:S(2)}) collective-permute-start(bf16[624,128]{1,0:T(8,128)(2,1)S(1)} %get-tuple-element.13), channel_id=1, source_target_pairs={{0,8},{2,10},{4,12},{6,14},{8,0},{10,2},{12,4},{14,6},{1,9},{3,11}... | collective-permute-start | bytes 479240 | tf_op jit(solution)/shard_map/ppermute | solution.py:397
  14.3 9.3 %collective-permute-start.3 = (bf16[624,128]{1,0:T(8,128)(2,1)S(1)}, bf16[624,128]{1,0:T(8,128)(2,1)S(1)}, u32[]{:S(2)}, u32[]{:S(2)}) collective-permute-start(bf16[624,128]{1,0:T(8,128)(2,1)S(1)} %get-tuple-element.14), channel_id=1, source_target_pairs={{0,12},{2,14},{4,0},{6,2},{8,4},{10,6},{12,8},{14,10},{1,13},{3,15... | collective-permute-start | bytes 479240 | tf_op jit(solution)/shard_map/ppermute | solution.py:397
  28.5 7.4 %collective-permute-start.6 = (bf16[96,512]{1,0:T(8,128)(2,1)S(1)}, bf16[96,512]{1,0:T(8,128)(2,1)S(1)}, u32[]{:S(2)}, u32[]{:S(2)}) collective-permute-start(bf16[96,512]{1,0:T(8,128)(2,1)S(1)} %smear.1.rest_0_), channel_id=1, source_target_pairs={{0,12},{2,14},{4,0},{6,2},{8,4},{10,6},{12,8},{14,10},{1,13},{3,15... | collective-permute-start | bytes 294920 | tf_op jit(solution)/shard_map/ppermute | solution.py:397
  33.5 6.5 %collective-permute-start.4 = (bf16[96,512]{1,0:T(8,128)(2,1)S(1)}, bf16[96,512]{1,0:T(8,128)(2,1)S(1)}, u32[]{:S(2)}, u32[]{:S(2)}) collective-permute-start(bf16[96,512]{1,0:T(8,128)(2,1)S(1)} %smear.1.rest_0_), channel_id=1, source_target_pairs={{0,4},{2,6},{4,8},{6,10},{8,12},{10,14},{12,0},{14,2},{1,5},{3,7},... | collective-permute-start | bytes 294920 | tf_op jit(solution)/shard_map/ppermute | solution.py:397
  33.5 9.4 %collective-permute-start.5 = (bf16[96,512]{1,0:T(8,128)(2,1)S(1)}, bf16[96,512]{1,0:T(8,128)(2,1)S(1)}, u32[]{:S(2)}, u32[]{:S(2)}) collective-permute-start(bf16[96,512]{1,0:T(8,128)(2,1)S(1)} %smear.1.rest_0_), channel_id=1, source_target_pairs={{0,8},{2,10},{4,12},{6,14},{8,0},{10,2},{12,4},{14,6},{1,9},{3,11}... | collective-permute-start | bytes 294920 | tf_op jit(solution)/shard_map/ppermute | solution.py:397
  34.1 11.1 %collective-permute-start.7 = (bf16[96,512]{1,0:T(8,128)(2,1)S(1)}, bf16[96,512]{1,0:T(8,128)(2,1)S(1)}, u32[]{:S(2)}, u32[]{:S(2)}) collective-permute-start(bf16[96,512]{1,0:T(8,128)(2,1)S(1)} %smear.1.rest_0_), channel_id=1, source_target_pairs={{0,2},{2,0},{4,6},{6,4},{8,10},{10,8},{12,14},{14,12},{1,3},{3,1},... | collective-permute-start | bytes 294920 | tf_op jit(solution)/shard_map/ppermute | solution.py:394
  35.9 9.3 %collective-permute-start.9 = (bf16[96,512]{1,0:T(8,128)(2,1)S(1)}, bf16[96,512]{1,0:T(8,128)(2,1)S(1)}, u32[]{:S(2)}, u32[]{:S(2)}) collective-permute-start(bf16[96,512]{1,0:T(8,128)(2,1)S(1)} %collective-permute-done.6.rest_3_), channel_id=1, source_target_pairs={{0,2},{2,0},{4,6},{6,4},{8,10},{10,8},{12,14},{14,12},{1,3},{3,1},... | collective-permute-start | bytes 294920 | tf_op jit(solution)/shard_map/ppermute | solution.py:394
  40.0 5.2 %collective-permute-start.8 = (bf16[96,512]{1,0:T(8,128)(2,1)S(1)}, bf16[96,512]{1,0:T(8,128)(2,1)S(1)}, u32[]{:S(2)}, u32[]{:S(2)}) collective-permute-start(bf16[96,512]{1,0:T(8,128)(2,1)S(1)} %collective-permute-done.4.rest_1_), channel_id=1, source_target_pairs={{0,2},{2,0},{4,6},{6,4},{8,10},{10,8},{12,14},{14,12},{1,3},{3,1},... | collective-permute-start | bytes 294920 | tf_op jit(solution)/shard_map/ppermute | solution.py:394
  42.9 4.6 %collective-permute-start.10 = (bf16[96,512]{1,0:T(8,128)(2,1)S(1)}, bf16[96,512]{1,0:T(8,128)(2,1)S(1)}, u32[]{:S(2)}, u32[]{:S(2)}) collective-permute-start(bf16[96,512]{1,0:T(8,128)(2,1)S(1)} %collective-permute-done.5.rest_2_), channel_id=1, source_target_pairs={{0,2},{2,0},{4,6},{6,4},{8,10},{10,8},{12,14},{14,12},{1,3},{3,1},... | collective-permute-start | bytes 294920 | tf_op jit(solution)/shard_map/ppermute | solution.py:394

commit v3 on v2

--- a/solution.py
+++ b/solution.py
@@ -181,7 +181,7 @@
                 window[part, 6:8, :] = narrow[4 * part : 4 * part + 2, :]
         windows[slab] = window[...].reshape(WINDOW, 128).astype(jnp.bfloat16)
     for hop in range(PLANES):
-        outs[hop][...] = windows[slab_of(lax.rem(z + hop, PLANES), h)]
+        outs[hop][...] = windows[slab_of(z ^ hop, h)]
 
 
 def by_color(part):
@@ -217,6 +217,9 @@
     at_start = x_place == 0
     low = lane < LX
 
+    z, _ = my_place()
+    up = 1 + 2 * lax.rem(z, 2)
+
     def scaled(part, value):
         return kappa_hop * (value + 1.0 if is_diagonal(part) else value)
 
@@ -257,8 +260,8 @@
 
     def one_step(source, target):
         def one(plane, carry):
-            above = lax.rem(plane + 3, PLANES)
-            below = lax.rem(plane + 1, PLANES)
+            above = lax.rem(plane + up, PLANES)
+            below = lax.rem(plane + PLANES - up, PLANES)
             for vector in range(FIELDS // 6):
                 base = vector * 6
                 field = [phi[source, plane, base + by_color(i)] for i in range(6)]
@@ -285,14 +288,14 @@
 
     last = NSMEAR % 2
     for plane in range(PLANES):
-        true_plane = lax.rem(my_place()[0] + PLANES - plane, PLANES)
+        true_plane = z ^ plane
         for row in range(4):
             flat[true_plane, :, row * 128 : (row + 1) * 128] = phi[last, plane, :, 2 + row, :]
     out[...] = flat[...].reshape(PLANES * FIELDS, 512).astype(jnp.bfloat16)
 
 
 def column_start(z, hop, side):
-    slab = slab_of(lax.rem(z + PLANES - hop, PLANES), side)
+    slab = slab_of(z ^ hop, side)
     return pl.ds(pl.multiple_of(slab * 512, 512), 512)
 
 
@@ -393,9 +396,11 @@
     def swapped(block):
         return lax.ppermute(block, "space", [(i, i ^ 1) for i in range(count)])
 
-    def moved_up(block, planes):
-        return lax.ppermute(block, "space", [(i, (i + 2 * planes) % count) for i in range(count)])
-
+    def across(block, hop):
+        return lax.ppermute(block, "space", [(i, i ^ 2 * hop) for i in range(count)])
+
+    far = solutions.reshape(FIELDS, 16, 128), links.reshape(LINKS, 16, 128)
+    far = [pltpu.with_memory_space_constraint(array, pltpu.HBM) for array in far]
     ends, wide = pl.pallas_call(
         read_kernel,
         out_shape=[
@@ -409,9 +414,9 @@
             pltpu.SemaphoreType.DMA(()),
             pltpu.SemaphoreType.DMA(()),
         ],
-        compiler_params=pltpu.CompilerParams(vmem_limit_bytes=63 * 1024 * 1024),
+        compiler_params=pltpu.CompilerParams(vmem_limit_bytes=16 * 1024 * 1024),
         name="read",
-    )(solutions.reshape(FIELDS, 16, 128), links.reshape(LINKS, 16, 128))
+    )(*far)
     packed = pl.pallas_call(
         pack_kernel,
         out_shape=[jax.ShapeDtypeStruct((WINDOW, 128), jnp.bfloat16)] * PLANES,
@@ -426,7 +431,7 @@
         name="pack",
     )(wide, swapped(ends))
     vectors = eigvecs.shape[1]
-    blocks = [packed[0]] + [moved_up(packed[hop], hop) for hop in range(1, PLANES)]
+    blocks = [packed[0]] + [across(packed[hop], hop) for hop in range(1, PLANES)]
     vectors = eigvecs.shape[1]
     block = pl.pallas_call(
         smear_kernel,
@@ -442,7 +447,7 @@
         cost_estimate=pl.CostEstimate(flops=10**9, bytes_accessed=2 * 10**7, transcendentals=0),
         name="smear",
     )(*blocks)
-    own = [block] + [moved_up(block, hop) for hop in range(1, PLANES)]
+    own = [block] + [across(block, hop) for hop in range(1, PLANES)]
     own[FAR] = lax.optimization_barrier((own[FAR], own[1], own[3]))[0]
     other = [swapped(part) for part in own]
     smeared = pl.pallas_call(

time: 48.8 us -> 45.5 us (0.932)
  starting transfers between devices: 20.7 us -> 17.9 us
  waiting for transfers between devices: 15.9 us -> 17.2 us
  local copies, waits for them, and re-layouts: 1.09 us -> 0.01 us
  Pallas kernels: 10.3 us -> 9.59 us
    ppermute x6, starting transfers between devices: 11.7 us -> 9.21 us  [across(): lax.ppermute(block, 'space', [(i, i ^ 2 * hop) for i in range(count)])]
    ppermute x6, waiting for transfers between devices: 12.3 us -> 13.6 us  [across(): lax.ppermute(block, 'space', [(i, i ^ 2 * hop) for i in range(count)])]
    unnamed x4 -> x2, local copies, waits for them, and re-layouts: 1.09 us -> 0.01 us
    pallas_call x1, Pallas kernels: 2.02 us -> 1.32 us  [in_slabs(): pl.pallas_call(read_kernel, out_shape=[jax.ShapeDtypeStruct((4 * PARTS, 1...]
  transfers between devices with their start and end apart: 11 -> 11, of which waited for: 7 -> 7; matrix products, arithmetic and copies ran while one was open for 0% -> 0% of each run, Pallas kernels for 4% -> 5%
where the time goes in v3:
time: 45.5 us; the launch traced here: 45.4 us
  starting transfers between devices  17.9 us (39%)
  waiting for transfers between devices  17.2 us (38%)
  Pallas kernels  9.59 us (21%)
  between operations  0.67 us (1%)
    ppermute x6, waiting for transfers between devices, across(): lax.ppermute(block, 'space', [(i, i ^ 2 * hop) for i in range(count)])  13.6 us
    ppermute x6, starting transfers between devices, across(): lax.ppermute(block, 'space', [(i, i ^ 2 * hop) for i in range(count)])  9.21 us
    ppermute x5, starting transfers between devices, swapped(): return lax.ppermute(block, 'space', [(i, i ^ 1) for i in range(count)])  8.7 us
    pallas_call x1, Pallas kernels, in_slabs(): pl.pallas_call(smear_kernel, out_shape=jax.ShapeDtypeStruct((PLANES * FIE...  4.78 us
    ppermute x5, waiting for transfers between devices, swapped(): return lax.ppermute(block, 'space', [(i, i ^ 1) for i in range(count)])  3.62 us
    pallas_call x1, Pallas kernels, in_slabs(): pl.pallas_call(read_kernel, out_shape=[jax.ShapeDtypeStruct((4 * PARTS, 1...  1.32 us
    pallas_call x1, Pallas kernels, in_slabs(): pl.pallas_call(project_near_kernel, out_shape=jax.ShapeDtypeStruct((8, ve...  1.32 us
    pallas_call x1, Pallas kernels, in_slabs(): pl.pallas_call(project_far_kernel, out_shape=jax.ShapeDtypeStruct((8, vec...  1.13 us
  transfers between devices with their start and end apart: 11, of which 7 were waited for; matrix products, arithmetic and copies ran while one was open for 0% of the time, Pallas kernels for 5%

profile of v3, /device:TPU:0, one launch (start us, length us, event | category | flops | bytes accessed | tf_op | source)
XLA Modules:
  0.0 45.4 jit_solution(343841174025385546)
XLA Ops:
  0.6 0.0 copy-start
  0.6 1.3 %read.1 = (bf16[312,128]{1,0:T(8,128)(2,1)S(1)}, f32[78,16,128]{2,1,0:T(8,128)S(1)}) custom-call(f32[24,16,128]{2,1,0:T(8,128)} %bitcast.14, f32[54,16,128]{2,1,0:T(8,128)} %bitcast.13), custom_call_target="tpu_custom_call" | custom-call | tf_op jit(solution)/shard_map/read/pallas_call | solution.py:404
  2.0 3.0 %collective-permute-start = (bf16[312,128]{1,0:T(8,128)(2,1)S(1)}, bf16[312,128]{1,0:T(8,128)(2,1)S(1)}, u32[]{:S(2)}, u32[]{:S(2)}) collective-permute-start(bf16[312,128]{1,0:T(8,128)(2,1)S(1)} %get-tuple-element.10), channel_id=1, source_target_pairs={{0,2},{2,0},{4,6},{6,4},{8,10},{10,8},{12,14},{14,12},{1,3},{3,1},... | collective-permute-start | bytes 239624 | tf_op jit(solution)/shard_map/ppermute | solution.py:397
  5.0 2.4 %collective-permute-done.ends = bf16[312,128]{1,0:T(8,128)(2,1)S(1)} collective-permute-done((bf16[312,128]{1,0:T(8,128)(2,1)S(1)}, bf16[312,128]{1,0:T(8,128)(2,1)S(1)}, u32[]{:S(2)}, u32[]{:S(2)}) %collective-permute-start) | collective-permute-done | bytes 79904 | tf_op jit(solution)/shard_map/ppermute | solution.py:397
  7.4 0.2 pack.1
  7.6 2.2 %collective-permute-start.1 = (bf16[624,128]{1,0:T(8,128)(2,1)S(1)}, bf16[624,128]{1,0:T(8,128)(2,1)S(1)}, u32[]{:S(2)}, u32[]{:S(2)}) collective-permute-start(bf16[624,128]{1,0:T(8,128)(2,1)S(1)} %get-tuple-element.12), channel_id=1, source_target_pairs={{0,4},{2,6},{4,0},{6,2},{8,12},{10,14},{12,8},{14,10},{1,5},{3,7},... | collective-permute-start | bytes 479240 | tf_op jit(solution)/shard_map/ppermute | solution.py:400
  9.8 2.6 %collective-permute-start.2 = (bf16[624,128]{1,0:T(8,128)(2,1)S(1)}, bf16[624,128]{1,0:T(8,128)(2,1)S(1)}, u32[]{:S(2)}, u32[]{:S(2)}) collective-permute-start(bf16[624,128]{1,0:T(8,128)(2,1)S(1)} %get-tuple-element.13), channel_id=1, source_target_pairs={{0,8},{2,10},{4,12},{6,14},{8,0},{10,2},{12,4},{14,6},{1,9},{3,11}... | collective-permute-start | bytes 479240 | tf_op jit(solution)/shard_map/ppermute | solution.py:400
  12.4 0.0 collective-permute-start.3
  12.4 2.5 %collective-permute-done.1.rest_1_ = bf16[624,128]{1,0:T(8,128)(2,1)S(1)} collective-permute-done((bf16[624,128]{1,0:T(8,128)(2,1)S(1)}, bf16[624,128]{1,0:T(8,128)(2,1)S(1)}, u32[]{:S(2)}, u32[]{:S(2)}) %collective-permute-start.1) | collective-permute-done | bytes 159776 | tf_op jit(solution)/shard_map/ppermute | solution.py:400
  14.9 8.8 %collective-permute-done.2.rest_2_ = bf16[624,128]{1,0:T(8,128)(2,1)S(1)} collective-permute-done((bf16[624,128]{1,0:T(8,128)(2,1)S(1)}, bf16[624,128]{1,0:T(8,128)(2,1)S(1)}, u32[]{:S(2)}, u32[]{:S(2)}) %collective-permute-start.2) | collective-permute-done | bytes 159776 | tf_op jit(solution)/shard_map/ppermute | solution.py:400
  23.7 0.0 collective-permute-done.3.rest_3_
  23.7 4.8 %smear.1.rest_0_ = bf16[96,512]{1,0:T(8,128)(2,1)S(1)} custom-call(bf16[624,128]{1,0:T(8,128)(2,1)S(1)} %get-tuple-element.11.rest_0_, bf16[624,128]{1,0:T(8,128)(2,1)S(1)} %collective-permute-done.1.rest_1_, bf16[624,128]{1,0:T(8,128)(2,1)S(1)} %collective-permute-done.2.rest_2_, bf16[624,128]{1,0:T(8,128)(2,1)S(1)} %collective-permute-done.3.rest_3_), custom_call_target="tpu_custom_call" | custom-call | flops 1000000000 | bytes 20000000 | tf_op jit(solution)/shard_map/smear/pallas_call | solution.py:436
  28.5 2.5 %collective-permute-start.6 = (bf16[96,512]{1,0:T(8,128)(2,1)S(1)}, bf16[96,512]{1,0:T(8,128)(2,1)S(1)}, u32[]{:S(2)}, u32[]{:S(2)}) collective-permute-start(bf16[96,512]{1,0:T(8,128)(2,1)S(1)} %smear.1.rest_0_), channel_id=1, source_target_pairs={{0,12},{2,14},{4,8},{6,10},{8,4},{10,6},{12,0},{14,2},{1,13},{3,15... | collective-permute-start | bytes 294920 | tf_op jit(solution)/shard_map/ppermute | solution.py:400
  31.0 1.4 %collective-permute-start.4 = (bf16[96,512]{1,0:T(8,128)(2,1)S(1)}, bf16[96,512]{1,0:T(8,128)(2,1)S(1)}, u32[]{:S(2)}, u32[]{:S(2)}) collective-permute-start(bf16[96,512]{1,0:T(8,128)(2,1)S(1)} %smear.1.rest_0_), channel_id=1, source_target_pairs={{0,4},{2,6},{4,0},{6,2},{8,12},{10,14},{12,8},{14,10},{1,5},{3,7},... | collective-permute-start | bytes 294920 | tf_op jit(solution)/shard_map/ppermute | solution.py:400
  32.4 0.5 %collective-permute-start.5 = (bf16[96,512]{1,0:T(8,128)(2,1)S(1)}, bf16[96,512]{1,0:T(8,128)(2,1)S(1)}, u32[]{:S(2)}, u32[]{:S(2)}) collective-permute-start(bf16[96,512]{1,0:T(8,128)(2,1)S(1)} %smear.1.rest_0_), channel_id=1, source_target_pairs={{0,8},{2,10},{4,12},{6,14},{8,0},{10,2},{12,4},{14,6},{1,9},{3,11}... | collective-permute-start | bytes 294920 | tf_op jit(solution)/shard_map/ppermute | solution.py:400
  33.0 1.4 %collective-permute-start.7 = (bf16[96,512]{1,0:T(8,128)(2,1)S(1)}, bf16[96,512]{1,0:T(8,128)(2,1)S(1)}, u32[]{:S(2)}, u32[]{:S(2)}) collective-permute-start(bf16[96,512]{1,0:T(8,128)(2,1)S(1)} %smear.1.rest_0_), channel_id=1, source_target_pairs={{0,2},{2,0},{4,6},{6,4},{8,10},{10,8},{12,14},{14,12},{1,3},{3,1},... | collective-permute-start | bytes 294920 | tf_op jit(solution)/shard_map/ppermute | solution.py:397
  34.4 1.1 %collective-permute-done.6.rest_3_ = bf16[96,512]{1,0:T(8,128)(2,1)S(1)} collective-permute-done((bf16[96,512]{1,0:T(8,128)(2,1)S(1)}, bf16[96,512]{1,0:T(8,128)(2,1)S(1)}, u32[]{:S(2)}, u32[]{:S(2)}) %collective-permute-start.6) | collective-permute-done | bytes 98336 | tf_op jit(solution)/shard_map/ppermute | solution.py:400
  35.5 1.4 %collective-permute-start.9 = (bf16[96,512]{1,0:T(8,128)(2,1)S(1)}, bf16[96,512]{1,0:T(8,128)(2,1)S(1)}, u32[]{:S(2)}, u32[]{:S(2)}) collective-permute-start(bf16[96,512]{1,0:T(8,128)(2,1)S(1)} %collective-permute-done.6.rest_3_), channel_id=1, source_target_pairs={{0,2},{2,0},{4,6},{6,4},{8,10},{10,8},{12,14},{14,12},{1,3},{3,1},... | collective-permute-start | bytes 294920 | tf_op jit(solution)/shard_map/ppermute | solution.py:397
  36.8 0.4 collective-permute-done.4.rest_1_
  37.3 1.5 %collective-permute-start.8 = (bf16[96,512]{1,0:T(8,128)(2,1)S(1)}, bf16[96,512]{1,0:T(8,128)(2,1)S(1)}, u32[]{:S(2)}, u32[]{:S(2)}) collective-permute-start(bf16[96,512]{1,0:T(8,128)(2,1)S(1)} %collective-permute-done.4.rest_1_), channel_id=1, source_target_pairs={{0,2},{2,0},{4,6},{6,4},{8,10},{10,8},{12,14},{14,12},{1,3},{3,1},... | collective-permute-start | bytes 294920 | tf_op jit(solution)/shard_map/ppermute | solution.py:397
  38.7 0.8 %collective-permute-done.5.rest_2_ = bf16[96,512]{1,0:T(8,128)(2,1)S(1)} collective-permute-done((bf16[96,512]{1,0:T(8,128)(2,1)S(1)}, bf16[96,512]{1,0:T(8,128)(2,1)S(1)}, u32[]{:S(2)}, u32[]{:S(2)}) %collective-permute-start.5) | collective-permute-done | bytes 98336 | tf_op jit(solution)/shard_map/ppermute | solution.py:400
  39.5 1.4 %collective-permute-start.10 = (bf16[96,512]{1,0:T(8,128)(2,1)S(1)}, bf16[96,512]{1,0:T(8,128)(2,1)S(1)}, u32[]{:S(2)}, u32[]{:S(2)}) collective-permute-start(bf16[96,512]{1,0:T(8,128)(2,1)S(1)} %collective-permute-done.5.rest_2_), channel_id=1, source_target_pairs={{0,2},{2,0},{4,6},{6,4},{8,10},{10,8},{12,14},{14,12},{1,3},{3,1},... | collective-permute-start | bytes 294920 | tf_op jit(solution)/shard_map/ppermute | solution.py:397
  40.9 0.8 %own_plane.1 = bf16[12,2,2048]{2,1,0:T(2,128)(2,1)} custom-call(bf16[96,512]{1,0:T(8,128)(2,1)S(1)} %smear.1.rest_0_, bf16[96,512]{1,0:T(8,128)(2,1)S(1)} %collective-permute-done.4.rest_1_, bf16[96,512]{1,0:T(8,128)(2,1)S(1)} %collective-permute-done.5.rest_2_, bf16[96,512]{1,0:T(8,128)(2,1)S(1)} %collective-permute-done.6.rest_3_), custom_call_target="tpu_custom_call" | custom-call | tf_op jit(solution)/shard_map/own_plane/pallas_call | solution.py:453
  41.7 0.0 collective-permute-done.7.rest_4_
  41.7 0.0 collective-permute-done.9.rest_6_
  41.7 1.2 %collective-permute-done.8.rest_5_ = bf16[96,512]{1,0:T(8,128)(2,1)S(1)} collective-permute-done((bf16[96,512]{1,0:T(8,128)(2,1)S(1)}, bf16[96,512]{1,0:T(8,128)(2,1)S(1)}, u32[]{:S(2)}, u32[]{:S(2)}) %collective-permute-start.8) | collective-permute-done | bytes 98336 | tf_op jit(solution)/shard_map/ppermute | solution.py:397
  42.9 0.0 copy-done
  42.9 1.3 %project_near.1.near = f32[8,16]{1,0:T(8,128)S(1)} custom-call(bf16[768,2048]{1,0:T(8,128)(2,1)S(1)} %bitcast.11, bf16[96,512]{1,0:T(8,128)(2,1)S(1)} %smear.1.rest_0_, bf16[96,512]{1,0:T(8,128)(2,1)S(1)} %collective-permute-done.4.rest_1_, bf16[96,512]{1,0:T(8,128)(2,1)S(1)} %collective-permute-done.5.rest_2_, ...), custom_call_target="tpu_custom_call" | custom-call | flops 1000000000 | bytes 4000000 | tf_op jit(solution)/shard_map/project_near/pallas_call | solution.py:463
  44.2 0.0 collective-permute-done.10.block
  44.2 1.1 %project_far.1 = f32[8,16]{1,0:T(8,128)} custom-call(bf16[768,2048]{1,0:T(8,128)(2,1)S(1)} %bitcast.12, f32[8,16]{1,0:T(8,128)S(1)} %project_near.1.near, bf16[96,512]{1,0:T(8,128)(2,1)S(1)} %collective-permute-done.10.block), custom_call_target="tpu_custom_call" | custom-call | tf_op jit(solution)/shard_map/project_far/pallas_call | solution.py:476
Async XLA Ops:
  0.6 42.3 %copy-start = (bf16[1,16,2,3,8,2048]{5,4,3,2,1,0:T(8,128)(2,1)S(1)}, bf16[1,16,2,3,8,2048]{5,4,3,2,1,0:T(8,128)(2,1)}, u32[]{:S(2)}) copy-start(bf16[1,16,2,3,8,2048]{5,4,3,2,1,0:T(8,128)(2,1)} %param.5) | copy-start | bytes 9437188
  2.0 5.4 %collective-permute-start = (bf16[312,128]{1,0:T(8,128)(2,1)S(1)}, bf16[312,128]{1,0:T(8,128)(2,1)S(1)}, u32[]{:S(2)}, u32[]{:S(2)}) collective-permute-start(bf16[312,128]{1,0:T(8,128)(2,1)S(1)} %get-tuple-element.10), channel_id=1, source_target_pairs={{0,2},{2,0},{4,6},{6,4},{8,10},{10,8},{12,14},{14,12},{1,3},{3,1},... | collective-permute-start | bytes 239624 | tf_op jit(solution)/shard_map/ppermute | solution.py:397
  7.6 7.3 %collective-permute-start.1 = (bf16[624,128]{1,0:T(8,128)(2,1)S(1)}, bf16[624,128]{1,0:T(8,128)(2,1)S(1)}, u32[]{:S(2)}, u32[]{:S(2)}) collective-permute-start(bf16[624,128]{1,0:T(8,128)(2,1)S(1)} %get-tuple-element.12), channel_id=1, source_target_pairs={{0,4},{2,6},{4,0},{6,2},{8,12},{10,14},{12,8},{14,10},{1,5},{3,7},... | collective-permute-start | bytes 479240 | tf_op jit(solution)/shard_map/ppermute | solution.py:400
  9.8 13.9 %collective-permute-start.2 = (bf16[624,128]{1,0:T(8,128)(2,1)S(1)}, bf16[624,128]{1,0:T(8,128)(2,1)S(1)}, u32[]{:S(2)}, u32[]{:S(2)}) collective-permute-start(bf16[624,128]{1,0:T(8,128)(2,1)S(1)} %get-tuple-element.13), channel_id=1, source_target_pairs={{0,8},{2,10},{4,12},{6,14},{8,0},{10,2},{12,4},{14,6},{1,9},{3,11}... | collective-permute-start | bytes 479240 | tf_op jit(solution)/shard_map/ppermute | solution.py:400
  12.4 11.3 %collective-permute-start.3 = (bf16[624,128]{1,0:T(8,128)(2,1)S(1)}, bf16[624,128]{1,0:T(8,128)(2,1)S(1)}, u32[]{:S(2)}, u32[]{:S(2)}) collective-permute-start(bf16[624,128]{1,0:T(8,128)(2,1)S(1)} %get-tuple-element.14), channel_id=1, source_target_pairs={{0,12},{2,14},{4,8},{6,10},{8,4},{10,6},{12,0},{14,2},{1,13},{3,15... | collective-permute-start | bytes 479240 | tf_op jit(solution)/shard_map/ppermute | solution.py:400
  28.5 7.0 %collective-permute-start.6 = (bf16[96,512]{1,0:T(8,128)(2,1)S(1)}, bf16[96,512]{1,0:T(8,128)(2,1)S(1)}, u32[]{:S(2)}, u32[]{:S(2)}) collective-permute-start(bf16[96,512]{1,0:T(8,128)(2,1)S(1)} %smear.1.rest_0_), channel_id=1, source_target_pairs={{0,12},{2,14},{4,8},{6,10},{8,4},{10,6},{12,0},{14,2},{1,13},{3,15... | collective-permute-start | bytes 294920 | tf_op jit(solution)/shard_map/ppermute | solution.py:400
  31.0 6.2 %collective-permute-start.4 = (bf16[96,512]{1,0:T(8,128)(2,1)S(1)}, bf16[96,512]{1,0:T(8,128)(2,1)S(1)}, u32[]{:S(2)}, u32[]{:S(2)}) collective-permute-start(bf16[96,512]{1,0:T(8,128)(2,1)S(1)} %smear.1.rest_0_), channel_id=1, source_target_pairs={{0,4},{2,6},{4,0},{6,2},{8,12},{10,14},{12,8},{14,10},{1,5},{3,7},... | collective-permute-start | bytes 294920 | tf_op jit(solution)/shard_map/ppermute | solution.py:400
  32.4 7.1 %collective-permute-start.5 = (bf16[96,512]{1,0:T(8,128)(2,1)S(1)}, bf16[96,512]{1,0:T(8,128)(2,1)S(1)}, u32[]{:S(2)}, u32[]{:S(2)}) collective-permute-start(bf16[96,512]{1,0:T(8,128)(2,1)S(1)} %smear.1.rest_0_), channel_id=1, source_target_pairs={{0,8},{2,10},{4,12},{6,14},{8,0},{10,2},{12,4},{14,6},{1,9},{3,11}... | collective-permute-start | bytes 294920 | tf_op jit(solution)/shard_map/ppermute | solution.py:400
  33.0 8.7 %collective-permute-start.7 = (bf16[96,512]{1,0:T(8,128)(2,1)S(1)}, bf16[96,512]{1,0:T(8,128)(2,1)S(1)}, u32[]{:S(2)}, u32[]{:S(2)}) collective-permute-start(bf16[96,512]{1,0:T(8,128)(2,1)S(1)} %smear.1.rest_0_), channel_id=1, source_target_pairs={{0,2},{2,0},{4,6},{6,4},{8,10},{10,8},{12,14},{14,12},{1,3},{3,1},... | collective-permute-start | bytes 294920 | tf_op jit(solution)/shard_map/ppermute | solution.py:397
  35.5 6.2 %collective-permute-start.9 = (bf16[96,512]{1,0:T(8,128)(2,1)S(1)}, bf16[96,512]{1,0:T(8,128)(2,1)S(1)}, u32[]{:S(2)}, u32[]{:S(2)}) collective-permute-start(bf16[96,512]{1,0:T(8,128)(2,1)S(1)} %collective-permute-done.6.rest_3_), channel_id=1, source_target_pairs={{0,2},{2,0},{4,6},{6,4},{8,10},{10,8},{12,14},{14,12},{1,3},{3,1},... | collective-permute-start | bytes 294920 | tf_op jit(solution)/shard_map/ppermute | solution.py:397
  37.3 5.6 %collective-permute-start.8 = (bf16[96,512]{1,0:T(8,128)(2,1)S(1)}, bf16[96,512]{1,0:T(8,128)(2,1)S(1)}, u32[]{:S(2)}, u32[]{:S(2)}) collective-permute-start(bf16[96,512]{1,0:T(8,128)(2,1)S(1)} %collective-permute-done.4.rest_1_), channel_id=1, source_target_pairs={{0,2},{2,0},{4,6},{6,4},{8,10},{10,8},{12,14},{14,12},{1,3},{3,1},... | collective-permute-start | bytes 294920 | tf_op jit(solution)/shard_map/ppermute | solution.py:397
  39.5 4.7 %collective-permute-start.10 = (bf16[96,512]{1,0:T(8,128)(2,1)S(1)}, bf16[96,512]{1,0:T(8,128)(2,1)S(1)}, u32[]{:S(2)}, u32[]{:S(2)}) collective-permute-start(bf16[96,512]{1,0:T(8,128)(2,1)S(1)} %collective-permute-done.5.rest_2_), channel_id=1, source_target_pairs={{0,2},{2,0},{4,6},{6,4},{8,10},{10,8},{12,14},{14,12},{1,3},{3,1},... | collective-permute-start | bytes 294920 | tf_op jit(solution)/shard_map/ppermute | solution.py:397

commit v4 on v3

--- a/solution.py
+++ b/solution.py
@@ -308,17 +308,24 @@
     out[...] = column[z].reshape(out.shape).astype(jnp.bfloat16)
 
 
-FAR = 2
-
-
-def reduce_sites(eigvecs, columns, sites, masks, vectors, sums):
+NEAR = (0, 1)
+FAR = (2, 3)
+
+
+def reduce_sites(eigvecs, pieces, masks, vectors, sums):
     count = 4
-    width = sites.shape[0]
     for group in range(eigvecs.shape[0] // (48 * count)):
-        rows = eigvecs[group * 48 * count : (group + 1) * 48 * count, columns]
-        product = lax.dot_general(
-            rows, sites[...], (((1,), (1,)), ((), ())), preferred_element_type=jnp.float32
-        ).reshape(count, 48, width)
+        rows = slice(group * 48 * count, (group + 1) * 48 * count)
+        product = None
+        for columns, sites in pieces:
+            term = lax.dot_general(
+                eigvecs[rows, columns],
+                sites[...],
+                (((1,), (1,)), ((), ())),
+                preferred_element_type=jnp.float32,
+            )
+            product = term if product is None else product + term
+        product = product.reshape(count, 48, product.shape[1])
         for part in range(2):
             sums[part, group * count : (group + 1) * count, :] = jnp.sum(
                 product * masks[part][None], axis=1
@@ -336,26 +343,28 @@
 
 
 def project_near_kernel(eigvecs, *rest):
-    own, other = rest[:PLANES], list(rest[PLANES : 2 * PLANES - 1])
-    coefficients, sites, sums = rest[2 * PLANES - 1 :]
-    other.insert(FAR, None)
+    own, other = rest[:PLANES], dict(zip(NEAR, rest[PLANES:]))
+    coefficients, sites, sums = rest[PLANES + len(NEAR) :]
     half = PLANES * FIELDS
     z, h = my_place()
     for hop in range(PLANES):
-        for blocks, side in ((own, h), (other, 1 - h)):
-            rows = pl.ds(pl.multiple_of(side * half, half), half)
-            here = jnp.zeros((half, 512), jnp.bfloat16) if blocks[hop] is None else blocks[hop][...]
-            sites[rows, column_start(z, hop, side)] = here
+        rows = pl.ds(pl.multiple_of(h * half, half), half)
+        sites[rows, column_start(z, hop, h)] = own[hop][...]
+        rows = pl.ds(pl.multiple_of((1 - h) * half, half), half)
+        here = other[hop][...] if hop in NEAR else jnp.zeros((half, 512), jnp.bfloat16)
+        sites[rows, column_start(z, hop, 1 - h)] = here
     masks, vectors = projection_masks(2 * half, 0)
-    parts = reduce_sites(eigvecs, slice(None), sites, masks, vectors, sums)
+    parts = reduce_sites(eigvecs, [(slice(None), sites)], masks, vectors, sums)
     for part in range(2):
         coefficients[4 * part : 4 * part + 4, :] = parts[part]
 
 
-def project_far_kernel(eigvecs, near, block, coefficients, sums):
+def project_far_kernel(eigvecs, near, *rest):
+    blocks, (coefficients, sums) = rest[: len(FAR)], rest[len(FAR) :]
     z, h = my_place()
     masks, vectors = projection_masks(PLANES * FIELDS, 1 - h)
-    parts = reduce_sites(eigvecs, column_start(z, FAR, 1 - h), block, masks, vectors, sums)
+    pieces = [(column_start(z, hop, 1 - h), block) for hop, block in zip(FAR, blocks)]
+    parts = reduce_sites(eigvecs, pieces, masks, vectors, sums)
     for part in range(2):
         rows = slice(4 * part, 4 * part + 4)
         coefficients[rows, :] = near[rows, :] + parts[part]
@@ -447,9 +456,11 @@
         cost_estimate=pl.CostEstimate(flops=10**9, bytes_accessed=2 * 10**7, transcendentals=0),
         name="smear",
     )(*blocks)
-    own = [block] + [across(block, hop) for hop in range(1, PLANES)]
-    own[FAR] = lax.optimization_barrier((own[FAR], own[1], own[3]))[0]
-    other = [swapped(part) for part in own]
+    own = [block, across(block, 1), across(block, 2)]
+    own.append(across(own[2], 1))
+    other = [swapped(part) for part in own[:2]]
+    other.append(swapped(lax.optimization_barrier((own[2], other[0]))[0]))
+    other.append(swapped(own[3]))
     smeared = pl.pallas_call(
         own_plane_kernel,
         out_shape=jax.ShapeDtypeStruct((FIELDS // 2, 2, 2048), jnp.bfloat16),
@@ -463,7 +474,7 @@
     near = pl.pallas_call(
         project_near_kernel,
         out_shape=jax.ShapeDtypeStruct((8, vectors), jnp.float32),
-        in_specs=in_vmem(2 * PLANES),
+        in_specs=in_vmem(1 + PLANES + len(NEAR)),
         out_specs=pl.BlockSpec(memory_space=pltpu.VMEM),
         scratch_shapes=[
             pltpu.VMEM((2 * PLANES * FIELDS, 2048), jnp.bfloat16),
@@ -472,16 +483,16 @@
         compiler_params=limit,
         cost_estimate=pl.CostEstimate(flops=10**9, bytes_accessed=4 * 10**6, transcendentals=0),
         name="project_near",
-    )(eigvecs, *own, *other[:FAR], *other[FAR + 1 :])
+    )(eigvecs, *own, *[other[hop] for hop in NEAR])
     coefficients = pl.pallas_call(
         project_far_kernel,
         out_shape=jax.ShapeDtypeStruct((8, vectors), jnp.float32),
-        in_specs=in_vmem(3),
+        in_specs=in_vmem(2 + len(FAR)),
         out_specs=pl.BlockSpec(memory_space=pltpu.VMEM),
         scratch_shapes=[pltpu.VMEM((2, vectors, PLANES * FIELDS), jnp.float32)],
         compiler_params=limit,
         name="project_far",
-    )(eigvecs, near, other[FAR])
+    )(eigvecs, near, *[other[hop] for hop in FAR])
     smeared = smeared.reshape(1, 4, 3, 2, 1, 2048).swapaxes(2, 3)
     return smeared, coefficients.T[None]
 

time: 45.5 us -> 45.4 us (level)
  waiting for transfers between devices: 17.2 us -> 16.7 us
    ppermute x6, starting transfers between devices: 9.21 us -> 9.81 us  [across(): lax.ppermute(block, 'space', [(i, i ^ 2 * hop) for i in range(count)])]
where the time goes in v4:
time: 45.4 us; the launch traced here: 45.2 us
  starting transfers between devices  18.1 us (40%)
  waiting for transfers between devices  16.7 us (37%)
  Pallas kernels  9.78 us (22%)
  between operations  0.67 us (1%)
    ppermute x6, waiting for transfers between devices, across(): lax.ppermute(block, 'space', [(i, i ^ 2 * hop) for i in range(count)])  13.3 us
    ppermute x6, starting transfers between devices, across(): lax.ppermute(block, 'space', [(i, i ^ 2 * hop) for i in range(count)])  9.81 us
    ppermute x5, starting transfers between devices, swapped(): return lax.ppermute(block, 'space', [(i, i ^ 1) for i in range(count)])  8.3 us
    pallas_call x1, Pallas kernels, in_slabs(): pl.pallas_call(smear_kernel, out_shape=jax.ShapeDtypeStruct((PLANES * FIE...  4.78 us
    ppermute x5, waiting for transfers between devices, swapped(): return lax.ppermute(block, 'space', [(i, i ^ 1) for i in range(count)])  3.32 us
    pallas_call x1, Pallas kernels, in_slabs(): pl.pallas_call(project_far_kernel, out_shape=jax.ShapeDtypeStruct((8, vec...  1.32 us
    pallas_call x1, Pallas kernels, in_slabs(): pl.pallas_call(project_near_kernel, out_shape=jax.ShapeDtypeStruct((8, ve...  1.32 us
    pallas_call x1, Pallas kernels, in_slabs(): pl.pallas_call(read_kernel, out_shape=[jax.ShapeDtypeStruct((4 * PARTS, 1...  1.32 us
  transfers between devices with their start and end apart: 11, of which 7 were waited for; matrix products, arithmetic and copies ran while one was open for 0% of the time, Pallas kernels for 5%

profile of v4, /device:TPU:0, one launch (start us, length us, event | category | flops | bytes accessed | tf_op | source)
XLA Modules:
  0.0 45.2 jit_solution(12341399306093968459)
XLA Ops:
  0.6 0.0 copy-start
  0.6 1.3 %read.1 = (bf16[312,128]{1,0:T(8,128)(2,1)S(1)}, f32[78,16,128]{2,1,0:T(8,128)S(1)}) custom-call(f32[24,16,128]{2,1,0:T(8,128)} %bitcast.14, f32[54,16,128]{2,1,0:T(8,128)} %bitcast.13), custom_call_target="tpu_custom_call" | custom-call | tf_op jit(solution)/shard_map/read/pallas_call | solution.py:413
  2.0 3.0 %collective-permute-start = (bf16[312,128]{1,0:T(8,128)(2,1)S(1)}, bf16[312,128]{1,0:T(8,128)(2,1)S(1)}, u32[]{:S(2)}, u32[]{:S(2)}) collective-permute-start(bf16[312,128]{1,0:T(8,128)(2,1)S(1)} %get-tuple-element.10), channel_id=1, source_target_pairs={{0,2},{2,0},{4,6},{6,4},{8,10},{10,8},{12,14},{14,12},{1,3},{3,1},... | collective-permute-start | bytes 239624 | tf_op jit(solution)/shard_map/ppermute | solution.py:406
  5.0 2.4 %collective-permute-done.ends = bf16[312,128]{1,0:T(8,128)(2,1)S(1)} collective-permute-done((bf16[312,128]{1,0:T(8,128)(2,1)S(1)}, bf16[312,128]{1,0:T(8,128)(2,1)S(1)}, u32[]{:S(2)}, u32[]{:S(2)}) %collective-permute-start) | collective-permute-done | bytes 79904 | tf_op jit(solution)/shard_map/ppermute | solution.py:406
  7.4 0.2 pack.1
  7.6 2.2 %collective-permute-start.1 = (bf16[624,128]{1,0:T(8,128)(2,1)S(1)}, bf16[624,128]{1,0:T(8,128)(2,1)S(1)}, u32[]{:S(2)}, u32[]{:S(2)}) collective-permute-start(bf16[624,128]{1,0:T(8,128)(2,1)S(1)} %get-tuple-element.12), channel_id=1, source_target_pairs={{0,4},{2,6},{4,0},{6,2},{8,12},{10,14},{12,8},{14,10},{1,5},{3,7},... | collective-permute-start | bytes 479240 | tf_op jit(solution)/shard_map/ppermute | solution.py:409
  9.8 2.6 %collective-permute-start.2 = (bf16[624,128]{1,0:T(8,128)(2,1)S(1)}, bf16[624,128]{1,0:T(8,128)(2,1)S(1)}, u32[]{:S(2)}, u32[]{:S(2)}) collective-permute-start(bf16[624,128]{1,0:T(8,128)(2,1)S(1)} %get-tuple-element.13), channel_id=1, source_target_pairs={{0,8},{2,10},{4,12},{6,14},{8,0},{10,2},{12,4},{14,6},{1,9},{3,11}... | collective-permute-start | bytes 479240 | tf_op jit(solution)/shard_map/ppermute | solution.py:409
  12.4 0.0 collective-permute-start.3
  12.4 2.5 %collective-permute-done.1.rest_1_ = bf16[624,128]{1,0:T(8,128)(2,1)S(1)} collective-permute-done((bf16[624,128]{1,0:T(8,128)(2,1)S(1)}, bf16[624,128]{1,0:T(8,128)(2,1)S(1)}, u32[]{:S(2)}, u32[]{:S(2)}) %collective-permute-start.1) | collective-permute-done | bytes 159776 | tf_op jit(solution)/shard_map/ppermute | solution.py:409
  14.9 8.8 %collective-permute-done.2.rest_2_ = bf16[624,128]{1,0:T(8,128)(2,1)S(1)} collective-permute-done((bf16[624,128]{1,0:T(8,128)(2,1)S(1)}, bf16[624,128]{1,0:T(8,128)(2,1)S(1)}, u32[]{:S(2)}, u32[]{:S(2)}) %collective-permute-start.2) | collective-permute-done | bytes 159776 | tf_op jit(solution)/shard_map/ppermute | solution.py:409
  23.7 0.0 collective-permute-done.3.rest_3_
  23.7 4.8 %smear.1.rest_0_ = bf16[96,512]{1,0:T(8,128)(2,1)S(1)} custom-call(bf16[624,128]{1,0:T(8,128)(2,1)S(1)} %get-tuple-element.11.rest_0_, bf16[624,128]{1,0:T(8,128)(2,1)S(1)} %collective-permute-done.1.rest_1_, bf16[624,128]{1,0:T(8,128)(2,1)S(1)} %collective-permute-done.2.rest_2_, bf16[624,128]{1,0:T(8,128)(2,1)S(1)} %collective-permute-done.3.rest_3_), custom_call_target="tpu_custom_call" | custom-call | flops 1000000000 | bytes 20000000 | tf_op jit(solution)/shard_map/smear/pallas_call | solution.py:445
  28.5 3.3 %collective-permute-start.5 = (bf16[96,512]{1,0:T(8,128)(2,1)S(1)}, bf16[96,512]{1,0:T(8,128)(2,1)S(1)}, u32[]{:S(2)}, u32[]{:S(2)}) collective-permute-start(bf16[96,512]{1,0:T(8,128)(2,1)S(1)} %smear.1.rest_0_), channel_id=1, source_target_pairs={{0,8},{2,10},{4,12},{6,14},{8,0},{10,2},{12,4},{14,6},{1,9},{3,11}... | collective-permute-start | bytes 294920 | tf_op jit(solution)/shard_map/ppermute | solution.py:409
  31.8 0.0 collective-permute-start.4
  31.9 1.5 %collective-permute-start.7 = (bf16[96,512]{1,0:T(8,128)(2,1)S(1)}, bf16[96,512]{1,0:T(8,128)(2,1)S(1)}, u32[]{:S(2)}, u32[]{:S(2)}) collective-permute-start(bf16[96,512]{1,0:T(8,128)(2,1)S(1)} %smear.1.rest_0_), channel_id=1, source_target_pairs={{0,2},{2,0},{4,6},{6,4},{8,10},{10,8},{12,14},{14,12},{1,3},{3,1},... | collective-permute-start | bytes 294920 | tf_op jit(solution)/shard_map/ppermute | solution.py:406
  33.3 1.3 %collective-permute-done.5.rest_2_ = bf16[96,512]{1,0:T(8,128)(2,1)S(1)} collective-permute-done((bf16[96,512]{1,0:T(8,128)(2,1)S(1)}, bf16[96,512]{1,0:T(8,128)(2,1)S(1)}, u32[]{:S(2)}, u32[]{:S(2)}) %collective-permute-start.5) | collective-permute-done | bytes 98336 | tf_op jit(solution)/shard_map/ppermute | solution.py:409
  34.7 1.7 %collective-permute-start.6 = (bf16[96,512]{1,0:T(8,128)(2,1)S(1)}, bf16[96,512]{1,0:T(8,128)(2,1)S(1)}, u32[]{:S(2)}, u32[]{:S(2)}) collective-permute-start(bf16[96,512]{1,0:T(8,128)(2,1)S(1)} %collective-permute-done.5.rest_2_), channel_id=1, source_target_pairs={{0,4},{2,6},{4,0},{6,2},{8,12},{10,14},{12,8},{14,10},{1,5},{3,7},... | collective-permute-start | bytes 294920 | tf_op jit(solution)/shard_map/ppermute | solution.py:409
  36.4 0.2 collective-permute-done.4.rest_1_
  36.5 1.5 %collective-permute-start.8 = (bf16[96,512]{1,0:T(8,128)(2,1)S(1)}, bf16[96,512]{1,0:T(8,128)(2,1)S(1)}, u32[]{:S(2)}, u32[]{:S(2)}) collective-permute-start(bf16[96,512]{1,0:T(8,128)(2,1)S(1)} %collective-permute-done.4.rest_1_), channel_id=1, source_target_pairs={{0,2},{2,0},{4,6},{6,4},{8,10},{10,8},{12,14},{14,12},{1,3},{3,1},... | collective-permute-start | bytes 294920 | tf_op jit(solution)/shard_map/ppermute | solution.py:406
  38.0 0.0 collective-permute-done.7.rest_4_
  38.0 0.7 %collective-permute-start.9 = (bf16[96,512]{1,0:T(8,128)(2,1)S(1)}, bf16[96,512]{1,0:T(8,128)(2,1)S(1)}, u32[]{:S(2)}, u32[]{:S(2)}) collective-permute-start(bf16[96,512]{1,0:T(8,128)(2,1)S(1)} %collective-permute-done.5.rest_2_), channel_id=1, source_target_pairs={{0,2},{2,0},{4,6},{6,4},{8,10},{10,8},{12,14},{14,12},{1,3},{3,1},... | collective-permute-start | bytes 294920 | tf_op jit(solution)/shard_map/ppermute | solution.py:406
  38.8 0.5 %collective-permute-done.6.rest_3_ = bf16[96,512]{1,0:T(8,128)(2,1)S(1)} collective-permute-done((bf16[96,512]{1,0:T(8,128)(2,1)S(1)}, bf16[96,512]{1,0:T(8,128)(2,1)S(1)}, u32[]{:S(2)}, u32[]{:S(2)}) %collective-permute-start.6) | collective-permute-done | bytes 98336 | tf_op jit(solution)/shard_map/ppermute | solution.py:409
  39.3 1.6 %collective-permute-start.10 = (bf16[96,512]{1,0:T(8,128)(2,1)S(1)}, bf16[96,512]{1,0:T(8,128)(2,1)S(1)}, u32[]{:S(2)}, u32[]{:S(2)}) collective-permute-start(bf16[96,512]{1,0:T(8,128)(2,1)S(1)} %collective-permute-done.6.rest_3_), channel_id=1, source_target_pairs={{0,2},{2,0},{4,6},{6,4},{8,10},{10,8},{12,14},{14,12},{1,3},{3,1},... | collective-permute-start | bytes 294920 | tf_op jit(solution)/shard_map/ppermute | solution.py:406
  40.8 0.8 %own_plane.1 = bf16[12,2,2048]{2,1,0:T(2,128)(2,1)} custom-call(bf16[96,512]{1,0:T(8,128)(2,1)S(1)} %smear.1.rest_0_, bf16[96,512]{1,0:T(8,128)(2,1)S(1)} %collective-permute-done.4.rest_1_, bf16[96,512]{1,0:T(8,128)(2,1)S(1)} %collective-permute-done.5.rest_2_, bf16[96,512]{1,0:T(8,128)(2,1)S(1)} %collective-permute-done.6.rest_3_), custom_call_target="tpu_custom_call" | custom-call | tf_op jit(solution)/shard_map/own_plane/pallas_call | solution.py:464
  41.6 0.0 collective-permute-done.8.rest_5_
  41.7 0.0 copy-done
  41.7 1.3 %project_near.1.near = f32[8,16]{1,0:T(8,128)S(1)} custom-call(bf16[768,2048]{1,0:T(8,128)(2,1)S(1)} %bitcast.11, bf16[96,512]{1,0:T(8,128)(2,1)S(1)} %smear.1.rest_0_, bf16[96,512]{1,0:T(8,128)(2,1)S(1)} %collective-permute-done.4.rest_1_, bf16[96,512]{1,0:T(8,128)(2,1)S(1)} %collective-permute-done.5.rest_2_, ...), custom_call_target="tpu_custom_call" | custom-call | flops 1000000000 | bytes 4000000 | tf_op jit(solution)/shard_map/project_near/pallas_call | solution.py:474
  43.0 0.0 collective-permute-done.9.rest_0_
  43.0 0.9 %collective-permute-done.10.rest_1_ = bf16[96,512]{1,0:T(8,128)(2,1)S(1)} collective-permute-done((bf16[96,512]{1,0:T(8,128)(2,1)S(1)}, bf16[96,512]{1,0:T(8,128)(2,1)S(1)}, u32[]{:S(2)}, u32[]{:S(2)}) %collective-permute-start.10) | collective-permute-done | bytes 98336 | tf_op jit(solution)/shard_map/ppermute | solution.py:406
  43.9 1.3 %project_far.1 = f32[8,16]{1,0:T(8,128)} custom-call(bf16[768,2048]{1,0:T(8,128)(2,1)S(1)} %bitcast.12, f32[8,16]{1,0:T(8,128)S(1)} %project_near.1.near, bf16[96,512]{1,0:T(8,128)(2,1)S(1)} %collective-permute-done.9.rest_0_, bf16[96,512]{1,0:T(8,128)(2,1)S(1)} %collective-permute-done.10.rest_1_), custom_call_target="tpu_custom_call" | custom-call | tf_op jit(solution)/shard_map/project_far/pallas_call | solution.py:487
Async XLA Ops:
  0.6 41.0 %copy-start = (bf16[1,16,2,3,8,2048]{5,4,3,2,1,0:T(8,128)(2,1)S(1)}, bf16[1,16,2,3,8,2048]{5,4,3,2,1,0:T(8,128)(2,1)}, u32[]{:S(2)}) copy-start(bf16[1,16,2,3,8,2048]{5,4,3,2,1,0:T(8,128)(2,1)} %param.5) | copy-start | bytes 9437188
  2.0 5.4 %collective-permute-start = (bf16[312,128]{1,0:T(8,128)(2,1)S(1)}, bf16[312,128]{1,0:T(8,128)(2,1)S(1)}, u32[]{:S(2)}, u32[]{:S(2)}) collective-permute-start(bf16[312,128]{1,0:T(8,128)(2,1)S(1)} %get-tuple-element.10), channel_id=1, source_target_pairs={{0,2},{2,0},{4,6},{6,4},{8,10},{10,8},{12,14},{14,12},{1,3},{3,1},... | collective-permute-start | bytes 239624 | tf_op jit(solution)/shard_map/ppermute | solution.py:406
  7.6 7.3 %collective-permute-start.1 = (bf16[624,128]{1,0:T(8,128)(2,1)S(1)}, bf16[624,128]{1,0:T(8,128)(2,1)S(1)}, u32[]{:S(2)}, u32[]{:S(2)}) collective-permute-start(bf16[624,128]{1,0:T(8,128)(2,1)S(1)} %get-tuple-element.12), channel_id=1, source_target_pairs={{0,4},{2,6},{4,0},{6,2},{8,12},{10,14},{12,8},{14,10},{1,5},{3,7},... | collective-permute-start | bytes 479240 | tf_op jit(solution)/shard_map/ppermute | solution.py:409
  9.8 13.9 %collective-permute-start.2 = (bf16[624,128]{1,0:T(8,128)(2,1)S(1)}, bf16[624,128]{1,0:T(8,128)(2,1)S(1)}, u32[]{:S(2)}, u32[]{:S(2)}) collective-permute-start(bf16[624,128]{1,0:T(8,128)(2,1)S(1)} %get-tuple-element.13), channel_id=1, source_target_pairs={{0,8},{2,10},{4,12},{6,14},{8,0},{10,2},{12,4},{14,6},{1,9},{3,11}... | collective-permute-start | bytes 479240 | tf_op jit(solution)/shard_map/ppermute | solution.py:409
  12.4 11.3 %collective-permute-start.3 = (bf16[624,128]{1,0:T(8,128)(2,1)S(1)}, bf16[624,128]{1,0:T(8,128)(2,1)S(1)}, u32[]{:S(2)}, u32[]{:S(2)}) collective-permute-start(bf16[624,128]{1,0:T(8,128)(2,1)S(1)} %get-tuple-element.14), channel_id=1, source_target_pairs={{0,12},{2,14},{4,8},{6,10},{8,4},{10,6},{12,0},{14,2},{1,13},{3,15... | collective-permute-start | bytes 479240 | tf_op jit(solution)/shard_map/ppermute | solution.py:409
  28.5 6.2 %collective-permute-start.5 = (bf16[96,512]{1,0:T(8,128)(2,1)S(1)}, bf16[96,512]{1,0:T(8,128)(2,1)S(1)}, u32[]{:S(2)}, u32[]{:S(2)}) collective-permute-start(bf16[96,512]{1,0:T(8,128)(2,1)S(1)} %smear.1.rest_0_), channel_id=1, source_target_pairs={{0,8},{2,10},{4,12},{6,14},{8,0},{10,2},{12,4},{14,6},{1,9},{3,11}... | collective-permute-start | bytes 294920 | tf_op jit(solution)/shard_map/ppermute | solution.py:409
  31.8 4.7 %collective-permute-start.4 = (bf16[96,512]{1,0:T(8,128)(2,1)S(1)}, bf16[96,512]{1,0:T(8,128)(2,1)S(1)}, u32[]{:S(2)}, u32[]{:S(2)}) collective-permute-start(bf16[96,512]{1,0:T(8,128)(2,1)S(1)} %smear.1.rest_0_), channel_id=1, source_target_pairs={{0,4},{2,6},{4,0},{6,2},{8,12},{10,14},{12,8},{14,10},{1,5},{3,7},... | collective-permute-start | bytes 294920 | tf_op jit(solution)/shard_map/ppermute | solution.py:409
  31.9 6.2 %collective-permute-start.7 = (bf16[96,512]{1,0:T(8,128)(2,1)S(1)}, bf16[96,512]{1,0:T(8,128)(2,1)S(1)}, u32[]{:S(2)}, u32[]{:S(2)}) collective-permute-start(bf16[96,512]{1,0:T(8,128)(2,1)S(1)} %smear.1.rest_0_), channel_id=1, source_target_pairs={{0,2},{2,0},{4,6},{6,4},{8,10},{10,8},{12,14},{14,12},{1,3},{3,1},... | collective-permute-start | bytes 294920 | tf_op jit(solution)/shard_map/ppermute | solution.py:406
  34.7 4.6 %collective-permute-start.6 = (bf16[96,512]{1,0:T(8,128)(2,1)S(1)}, bf16[96,512]{1,0:T(8,128)(2,1)S(1)}, u32[]{:S(2)}, u32[]{:S(2)}) collective-permute-start(bf16[96,512]{1,0:T(8,128)(2,1)S(1)} %collective-permute-done.5.rest_2_), channel_id=1, source_target_pairs={{0,4},{2,6},{4,0},{6,2},{8,12},{10,14},{12,8},{14,10},{1,5},{3,7},... | collective-permute-start | bytes 294920 | tf_op jit(solution)/shard_map/ppermute | solution.py:409
  36.5 5.1 %collective-permute-start.8 = (bf16[96,512]{1,0:T(8,128)(2,1)S(1)}, bf16[96,512]{1,0:T(8,128)(2,1)S(1)}, u32[]{:S(2)}, u32[]{:S(2)}) collective-permute-start(bf16[96,512]{1,0:T(8,128)(2,1)S(1)} %collective-permute-done.4.rest_1_), channel_id=1, source_target_pairs={{0,2},{2,0},{4,6},{6,4},{8,10},{10,8},{12,14},{14,12},{1,3},{3,1},... | collective-permute-start | bytes 294920 | tf_op jit(solution)/shard_map/ppermute | solution.py:406
  38.0 4.9 %collective-permute-start.9 = (bf16[96,512]{1,0:T(8,128)(2,1)S(1)}, bf16[96,512]{1,0:T(8,128)(2,1)S(1)}, u32[]{:S(2)}, u32[]{:S(2)}) collective-permute-start(bf16[96,512]{1,0:T(8,128)(2,1)S(1)} %collective-permute-done.5.rest_2_), channel_id=1, source_target_pairs={{0,2},{2,0},{4,6},{6,4},{8,10},{10,8},{12,14},{14,12},{1,3},{3,1},... | collective-permute-start | bytes 294920 | tf_op jit(solution)/shard_map/ppermute | solution.py:406
  39.3 4.6 %collective-permute-start.10 = (bf16[96,512]{1,0:T(8,128)(2,1)S(1)}, bf16[96,512]{1,0:T(8,128)(2,1)S(1)}, u32[]{:S(2)}, u32[]{:S(2)}) collective-permute-start(bf16[96,512]{1,0:T(8,128)(2,1)S(1)} %collective-permute-done.6.rest_3_), channel_id=1, source_target_pairs={{0,2},{2,0},{4,6},{6,4},{8,10},{10,8},{12,14},{14,12},{1,3},{3,1},... | collective-permute-start | bytes 294920 | tf_op jit(solution)/shard_map/ppermute | solution.py:406

commit v5 on v4

--- a/solution.py
+++ b/solution.py
@@ -313,7 +313,7 @@
 
 
 def reduce_sites(eigvecs, pieces, masks, vectors, sums):
-    count = 4
+    count = 8
     for group in range(eigvecs.shape[0] // (48 * count)):
         rows = slice(group * 48 * count, (group + 1) * 48 * count)
         product = None
@@ -499,7 +499,7 @@
 
 def local(solutions, links, eigvecs):
     fits = lax.axis_size("space") == 2 * PLANES and solutions.shape[:2] == (1, 4)
-    fits = fits and solutions.shape[4:] == (1, 2048) and eigvecs.shape[1] % 4 == 0
+    fits = fits and solutions.shape[4:] == (1, 2048) and eigvecs.shape[1] % 8 == 0
     return (in_slabs if fits else by_planes)(solutions, links, eigvecs)
 
 

time: 45.4 us -> 45.4 us (level)
  no operation moved by 1% of the time
where the time goes in v5:
time: 45.4 us; the launch traced here: 45.2 us
  starting transfers between devices  18.1 us (40%)
  waiting for transfers between devices  16.7 us (37%)
  Pallas kernels  9.76 us (21%)
  between operations  0.67 us (1%)
    ppermute x6, waiting for transfers between devices, across(): lax.ppermute(block, 'space', [(i, i ^ 2 * hop) for i in range(count)])  13.3 us
    ppermute x6, starting transfers between devices, across(): lax.ppermute(block, 'space', [(i, i ^ 2 * hop) for i in range(count)])  9.81 us
    ppermute x5, starting transfers between devices, swapped(): return lax.ppermute(block, 'space', [(i, i ^ 1) for i in range(count)])  8.3 us
    pallas_call x1, Pallas kernels, in_slabs(): pl.pallas_call(smear_kernel, out_shape=jax.ShapeDtypeStruct((PLANES * FIE...  4.78 us
    ppermute x5, waiting for transfers between devices, swapped(): return lax.ppermute(block, 'space', [(i, i ^ 1) for i in range(count)])  3.34 us
    pallas_call x1, Pallas kernels, in_slabs(): pl.pallas_call(project_far_kernel, out_shape=jax.ShapeDtypeStruct((8, vec...  1.32 us
    pallas_call x1, Pallas kernels, in_slabs(): pl.pallas_call(read_kernel, out_shape=[jax.ShapeDtypeStruct((4 * PARTS, 1...  1.32 us
    pallas_call x1, Pallas kernels, in_slabs(): pl.pallas_call(project_near_kernel, out_shape=jax.ShapeDtypeStruct((8, ve...  1.3 us
  transfers between devices with their start and end apart: 11, of which 7 were waited for; matrix products, arithmetic and copies ran while one was open for 0% of the time, Pallas kernels for 5%

profile of v5, /device:TPU:0, one launch (start us, length us, event | category | flops | bytes accessed | tf_op | source)
XLA Modules:
  0.0 45.2 jit_solution(2217187001763208497)
XLA Ops:
  0.6 0.0 copy-start
  0.6 1.3 %read.1 = (bf16[312,128]{1,0:T(8,128)(2,1)S(1)}, f32[78,16,128]{2,1,0:T(8,128)S(1)}) custom-call(f32[24,16,128]{2,1,0:T(8,128)} %bitcast.14, f32[54,16,128]{2,1,0:T(8,128)} %bitcast.13), custom_call_target="tpu_custom_call" | custom-call | tf_op jit(solution)/shard_map/read/pallas_call | solution.py:413
  2.0 3.0 %collective-permute-start = (bf16[312,128]{1,0:T(8,128)(2,1)S(1)}, bf16[312,128]{1,0:T(8,128)(2,1)S(1)}, u32[]{:S(2)}, u32[]{:S(2)}) collective-permute-start(bf16[312,128]{1,0:T(8,128)(2,1)S(1)} %get-tuple-element.10), channel_id=1, source_target_pairs={{0,2},{2,0},{4,6},{6,4},{8,10},{10,8},{12,14},{14,12},{1,3},{3,1},... | collective-permute-start | bytes 239624 | tf_op jit(solution)/shard_map/ppermute | solution.py:406
  5.0 2.4 %collective-permute-done.ends = bf16[312,128]{1,0:T(8,128)(2,1)S(1)} collective-permute-done((bf16[312,128]{1,0:T(8,128)(2,1)S(1)}, bf16[312,128]{1,0:T(8,128)(2,1)S(1)}, u32[]{:S(2)}, u32[]{:S(2)}) %collective-permute-start) | collective-permute-done | bytes 79904 | tf_op jit(solution)/shard_map/ppermute | solution.py:406
  7.4 0.2 pack.1
  7.6 2.2 %collective-permute-start.1 = (bf16[624,128]{1,0:T(8,128)(2,1)S(1)}, bf16[624,128]{1,0:T(8,128)(2,1)S(1)}, u32[]{:S(2)}, u32[]{:S(2)}) collective-permute-start(bf16[624,128]{1,0:T(8,128)(2,1)S(1)} %get-tuple-element.12), channel_id=1, source_target_pairs={{0,4},{2,6},{4,0},{6,2},{8,12},{10,14},{12,8},{14,10},{1,5},{3,7},... | collective-permute-start | bytes 479240 | tf_op jit(solution)/shard_map/ppermute | solution.py:409
  9.8 2.6 %collective-permute-start.2 = (bf16[624,128]{1,0:T(8,128)(2,1)S(1)}, bf16[624,128]{1,0:T(8,128)(2,1)S(1)}, u32[]{:S(2)}, u32[]{:S(2)}) collective-permute-start(bf16[624,128]{1,0:T(8,128)(2,1)S(1)} %get-tuple-element.13), channel_id=1, source_target_pairs={{0,8},{2,10},{4,12},{6,14},{8,0},{10,2},{12,4},{14,6},{1,9},{3,11}... | collective-permute-start | bytes 479240 | tf_op jit(solution)/shard_map/ppermute | solution.py:409
  12.4 0.0 collective-permute-start.3
  12.4 2.5 %collective-permute-done.1.rest_1_ = bf16[624,128]{1,0:T(8,128)(2,1)S(1)} collective-permute-done((bf16[624,128]{1,0:T(8,128)(2,1)S(1)}, bf16[624,128]{1,0:T(8,128)(2,1)S(1)}, u32[]{:S(2)}, u32[]{:S(2)}) %collective-permute-start.1) | collective-permute-done | bytes 159776 | tf_op jit(solution)/shard_map/ppermute | solution.py:409
  14.9 8.8 %collective-permute-done.2.rest_2_ = bf16[624,128]{1,0:T(8,128)(2,1)S(1)} collective-permute-done((bf16[624,128]{1,0:T(8,128)(2,1)S(1)}, bf16[624,128]{1,0:T(8,128)(2,1)S(1)}, u32[]{:S(2)}, u32[]{:S(2)}) %collective-permute-start.2) | collective-permute-done | bytes 159776 | tf_op jit(solution)/shard_map/ppermute | solution.py:409
  23.7 0.0 collective-permute-done.3.rest_3_
  23.7 4.8 %smear.1.rest_0_ = bf16[96,512]{1,0:T(8,128)(2,1)S(1)} custom-call(bf16[624,128]{1,0:T(8,128)(2,1)S(1)} %get-tuple-element.11.rest_0_, bf16[624,128]{1,0:T(8,128)(2,1)S(1)} %collective-permute-done.1.rest_1_, bf16[624,128]{1,0:T(8,128)(2,1)S(1)} %collective-permute-done.2.rest_2_, bf16[624,128]{1,0:T(8,128)(2,1)S(1)} %collective-permute-done.3.rest_3_), custom_call_target="tpu_custom_call" | custom-call | flops 1000000000 | bytes 20000000 | tf_op jit(solution)/shard_map/smear/pallas_call | solution.py:445
  28.5 3.3 %collective-permute-start.5 = (bf16[96,512]{1,0:T(8,128)(2,1)S(1)}, bf16[96,512]{1,0:T(8,128)(2,1)S(1)}, u32[]{:S(2)}, u32[]{:S(2)}) collective-permute-start(bf16[96,512]{1,0:T(8,128)(2,1)S(1)} %smear.1.rest_0_), channel_id=1, source_target_pairs={{0,8},{2,10},{4,12},{6,14},{8,0},{10,2},{12,4},{14,6},{1,9},{3,11}... | collective-permute-start | bytes 294920 | tf_op jit(solution)/shard_map/ppermute | solution.py:409
  31.8 0.0 collective-permute-start.4
  31.9 1.5 %collective-permute-start.7 = (bf16[96,512]{1,0:T(8,128)(2,1)S(1)}, bf16[96,512]{1,0:T(8,128)(2,1)S(1)}, u32[]{:S(2)}, u32[]{:S(2)}) collective-permute-start(bf16[96,512]{1,0:T(8,128)(2,1)S(1)} %smear.1.rest_0_), channel_id=1, source_target_pairs={{0,2},{2,0},{4,6},{6,4},{8,10},{10,8},{12,14},{14,12},{1,3},{3,1},... | collective-permute-start | bytes 294920 | tf_op jit(solution)/shard_map/ppermute | solution.py:406
  33.3 1.3 %collective-permute-done.5.rest_2_ = bf16[96,512]{1,0:T(8,128)(2,1)S(1)} collective-permute-done((bf16[96,512]{1,0:T(8,128)(2,1)S(1)}, bf16[96,512]{1,0:T(8,128)(2,1)S(1)}, u32[]{:S(2)}, u32[]{:S(2)}) %collective-permute-start.5) | collective-permute-done | bytes 98336 | tf_op jit(solution)/shard_map/ppermute | solution.py:409
  34.7 1.7 %collective-permute-start.6 = (bf16[96,512]{1,0:T(8,128)(2,1)S(1)}, bf16[96,512]{1,0:T(8,128)(2,1)S(1)}, u32[]{:S(2)}, u32[]{:S(2)}) collective-permute-start(bf16[96,512]{1,0:T(8,128)(2,1)S(1)} %collective-permute-done.5.rest_2_), channel_id=1, source_target_pairs={{0,4},{2,6},{4,0},{6,2},{8,12},{10,14},{12,8},{14,10},{1,5},{3,7},... | collective-permute-start | bytes 294920 | tf_op jit(solution)/shard_map/ppermute | solution.py:409
  36.4 0.2 collective-permute-done.4.rest_1_
  36.5 1.5 %collective-permute-start.8 = (bf16[96,512]{1,0:T(8,128)(2,1)S(1)}, bf16[96,512]{1,0:T(8,128)(2,1)S(1)}, u32[]{:S(2)}, u32[]{:S(2)}) collective-permute-start(bf16[96,512]{1,0:T(8,128)(2,1)S(1)} %collective-permute-done.4.rest_1_), channel_id=1, source_target_pairs={{0,2},{2,0},{4,6},{6,4},{8,10},{10,8},{12,14},{14,12},{1,3},{3,1},... | collective-permute-start | bytes 294920 | tf_op jit(solution)/shard_map/ppermute | solution.py:406
  38.0 0.0 collective-permute-done.7.rest_4_
  38.0 0.7 %collective-permute-start.9 = (bf16[96,512]{1,0:T(8,128)(2,1)S(1)}, bf16[96,512]{1,0:T(8,128)(2,1)S(1)}, u32[]{:S(2)}, u32[]{:S(2)}) collective-permute-start(bf16[96,512]{1,0:T(8,128)(2,1)S(1)} %collective-permute-done.5.rest_2_), channel_id=1, source_target_pairs={{0,2},{2,0},{4,6},{6,4},{8,10},{10,8},{12,14},{14,12},{1,3},{3,1},... | collective-permute-start | bytes 294920 | tf_op jit(solution)/shard_map/ppermute | solution.py:406
  38.8 0.5 %collective-permute-done.6.rest_3_ = bf16[96,512]{1,0:T(8,128)(2,1)S(1)} collective-permute-done((bf16[96,512]{1,0:T(8,128)(2,1)S(1)}, bf16[96,512]{1,0:T(8,128)(2,1)S(1)}, u32[]{:S(2)}, u32[]{:S(2)}) %collective-permute-start.6) | collective-permute-done | bytes 98336 | tf_op jit(solution)/shard_map/ppermute | solution.py:409
  39.3 1.6 %collective-permute-start.10 = (bf16[96,512]{1,0:T(8,128)(2,1)S(1)}, bf16[96,512]{1,0:T(8,128)(2,1)S(1)}, u32[]{:S(2)}, u32[]{:S(2)}) collective-permute-start(bf16[96,512]{1,0:T(8,128)(2,1)S(1)} %collective-permute-done.6.rest_3_), channel_id=1, source_target_pairs={{0,2},{2,0},{4,6},{6,4},{8,10},{10,8},{12,14},{14,12},{1,3},{3,1},... | collective-permute-start | bytes 294920 | tf_op jit(solution)/shard_map/ppermute | solution.py:406
  40.8 0.8 %own_plane.1 = bf16[12,2,2048]{2,1,0:T(2,128)(2,1)} custom-call(bf16[96,512]{1,0:T(8,128)(2,1)S(1)} %smear.1.rest_0_, bf16[96,512]{1,0:T(8,128)(2,1)S(1)} %collective-permute-done.4.rest_1_, bf16[96,512]{1,0:T(8,128)(2,1)S(1)} %collective-permute-done.5.rest_2_, bf16[96,512]{1,0:T(8,128)(2,1)S(1)} %collective-permute-done.6.rest_3_), custom_call_target="tpu_custom_call" | custom-call | tf_op jit(solution)/shard_map/own_plane/pallas_call | solution.py:464
  41.6 0.0 collective-permute-done.8.rest_5_
  41.7 0.0 copy-done
  41.7 1.3 %project_near.1.near = f32[8,16]{1,0:T(8,128)S(1)} custom-call(bf16[768,2048]{1,0:T(8,128)(2,1)S(1)} %bitcast.11, bf16[96,512]{1,0:T(8,128)(2,1)S(1)} %smear.1.rest_0_, bf16[96,512]{1,0:T(8,128)(2,1)S(1)} %collective-permute-done.4.rest_1_, bf16[96,512]{1,0:T(8,128)(2,1)S(1)} %collective-permute-done.5.rest_2_, ...), custom_call_target="tpu_custom_call" | custom-call | flops 1000000000 | bytes 4000000 | tf_op jit(solution)/shard_map/project_near/pallas_call | solution.py:474
  43.0 0.0 collective-permute-done.9.rest_0_
  43.0 0.9 %collective-permute-done.10.rest_1_ = bf16[96,512]{1,0:T(8,128)(2,1)S(1)} collective-permute-done((bf16[96,512]{1,0:T(8,128)(2,1)S(1)}, bf16[96,512]{1,0:T(8,128)(2,1)S(1)}, u32[]{:S(2)}, u32[]{:S(2)}) %collective-permute-start.10) | collective-permute-done | bytes 98336 | tf_op jit(solution)/shard_map/ppermute | solution.py:406
  43.9 1.3 %project_far.1 = f32[8,16]{1,0:T(8,128)} custom-call(bf16[768,2048]{1,0:T(8,128)(2,1)S(1)} %bitcast.12, f32[8,16]{1,0:T(8,128)S(1)} %project_near.1.near, bf16[96,512]{1,0:T(8,128)(2,1)S(1)} %collective-permute-done.9.rest_0_, bf16[96,512]{1,0:T(8,128)(2,1)S(1)} %collective-permute-done.10.rest_1_), custom_call_target="tpu_custom_call" | custom-call | tf_op jit(solution)/shard_map/project_far/pallas_call | solution.py:487
Async XLA Ops:
  0.6 41.0 %copy-start = (bf16[1,16,2,3,8,2048]{5,4,3,2,1,0:T(8,128)(2,1)S(1)}, bf16[1,16,2,3,8,2048]{5,4,3,2,1,0:T(8,128)(2,1)}, u32[]{:S(2)}) copy-start(bf16[1,16,2,3,8,2048]{5,4,3,2,1,0:T(8,128)(2,1)} %param.5) | copy-start | bytes 9437188
  2.0 5.4 %collective-permute-start = (bf16[312,128]{1,0:T(8,128)(2,1)S(1)}, bf16[312,128]{1,0:T(8,128)(2,1)S(1)}, u32[]{:S(2)}, u32[]{:S(2)}) collective-permute-start(bf16[312,128]{1,0:T(8,128)(2,1)S(1)} %get-tuple-element.10), channel_id=1, source_target_pairs={{0,2},{2,0},{4,6},{6,4},{8,10},{10,8},{12,14},{14,12},{1,3},{3,1},... | collective-permute-start | bytes 239624 | tf_op jit(solution)/shard_map/ppermute | solution.py:406
  7.6 7.3 %collective-permute-start.1 = (bf16[624,128]{1,0:T(8,128)(2,1)S(1)}, bf16[624,128]{1,0:T(8,128)(2,1)S(1)}, u32[]{:S(2)}, u32[]{:S(2)}) collective-permute-start(bf16[624,128]{1,0:T(8,128)(2,1)S(1)} %get-tuple-element.12), channel_id=1, source_target_pairs={{0,4},{2,6},{4,0},{6,2},{8,12},{10,14},{12,8},{14,10},{1,5},{3,7},... | collective-permute-start | bytes 479240 | tf_op jit(solution)/shard_map/ppermute | solution.py:409
  9.8 13.9 %collective-permute-start.2 = (bf16[624,128]{1,0:T(8,128)(2,1)S(1)}, bf16[624,128]{1,0:T(8,128)(2,1)S(1)}, u32[]{:S(2)}, u32[]{:S(2)}) collective-permute-start(bf16[624,128]{1,0:T(8,128)(2,1)S(1)} %get-tuple-element.13), channel_id=1, source_target_pairs={{0,8},{2,10},{4,12},{6,14},{8,0},{10,2},{12,4},{14,6},{1,9},{3,11}... | collective-permute-start | bytes 479240 | tf_op jit(solution)/shard_map/ppermute | solution.py:409
  12.4 11.3 %collective-permute-start.3 = (bf16[624,128]{1,0:T(8,128)(2,1)S(1)}, bf16[624,128]{1,0:T(8,128)(2,1)S(1)}, u32[]{:S(2)}, u32[]{:S(2)}) collective-permute-start(bf16[624,128]{1,0:T(8,128)(2,1)S(1)} %get-tuple-element.14), channel_id=1, source_target_pairs={{0,12},{2,14},{4,8},{6,10},{8,4},{10,6},{12,0},{14,2},{1,13},{3,15... | collective-permute-start | bytes 479240 | tf_op jit(solution)/shard_map/ppermute | solution.py:409
  28.5 6.2 %collective-permute-start.5 = (bf16[96,512]{1,0:T(8,128)(2,1)S(1)}, bf16[96,512]{1,0:T(8,128)(2,1)S(1)}, u32[]{:S(2)}, u32[]{:S(2)}) collective-permute-start(bf16[96,512]{1,0:T(8,128)(2,1)S(1)} %smear.1.rest_0_), channel_id=1, source_target_pairs={{0,8},{2,10},{4,12},{6,14},{8,0},{10,2},{12,4},{14,6},{1,9},{3,11}... | collective-permute-start | bytes 294920 | tf_op jit(solution)/shard_map/ppermute | solution.py:409
  31.8 4.7 %collective-permute-start.4 = (bf16[96,512]{1,0:T(8,128)(2,1)S(1)}, bf16[96,512]{1,0:T(8,128)(2,1)S(1)}, u32[]{:S(2)}, u32[]{:S(2)}) collective-permute-start(bf16[96,512]{1,0:T(8,128)(2,1)S(1)} %smear.1.rest_0_), channel_id=1, source_target_pairs={{0,4},{2,6},{4,0},{6,2},{8,12},{10,14},{12,8},{14,10},{1,5},{3,7},... | collective-permute-start | bytes 294920 | tf_op jit(solution)/shard_map/ppermute | solution.py:409
  31.9 6.2 %collective-permute-start.7 = (bf16[96,512]{1,0:T(8,128)(2,1)S(1)}, bf16[96,512]{1,0:T(8,128)(2,1)S(1)}, u32[]{:S(2)}, u32[]{:S(2)}) collective-permute-start(bf16[96,512]{1,0:T(8,128)(2,1)S(1)} %smear.1.rest_0_), channel_id=1, source_target_pairs={{0,2},{2,0},{4,6},{6,4},{8,10},{10,8},{12,14},{14,12},{1,3},{3,1},... | collective-permute-start | bytes 294920 | tf_op jit(solution)/shard_map/ppermute | solution.py:406
  34.7 4.6 %collective-permute-start.6 = (bf16[96,512]{1,0:T(8,128)(2,1)S(1)}, bf16[96,512]{1,0:T(8,128)(2,1)S(1)}, u32[]{:S(2)}, u32[]{:S(2)}) collective-permute-start(bf16[96,512]{1,0:T(8,128)(2,1)S(1)} %collective-permute-done.5.rest_2_), channel_id=1, source_target_pairs={{0,4},{2,6},{4,0},{6,2},{8,12},{10,14},{12,8},{14,10},{1,5},{3,7},... | collective-permute-start | bytes 294920 | tf_op jit(solution)/shard_map/ppermute | solution.py:409
  36.5 5.1 %collective-permute-start.8 = (bf16[96,512]{1,0:T(8,128)(2,1)S(1)}, bf16[96,512]{1,0:T(8,128)(2,1)S(1)}, u32[]{:S(2)}, u32[]{:S(2)}) collective-permute-start(bf16[96,512]{1,0:T(8,128)(2,1)S(1)} %collective-permute-done.4.rest_1_), channel_id=1, source_target_pairs={{0,2},{2,0},{4,6},{6,4},{8,10},{10,8},{12,14},{14,12},{1,3},{3,1},... | collective-permute-start | bytes 294920 | tf_op jit(solution)/shard_map/ppermute | solution.py:406
  38.0 4.9 %collective-permute-start.9 = (bf16[96,512]{1,0:T(8,128)(2,1)S(1)}, bf16[96,512]{1,0:T(8,128)(2,1)S(1)}, u32[]{:S(2)}, u32[]{:S(2)}) collective-permute-start(bf16[96,512]{1,0:T(8,128)(2,1)S(1)} %collective-permute-done.5.rest_2_), channel_id=1, source_target_pairs={{0,2},{2,0},{4,6},{6,4},{8,10},{10,8},{12,14},{14,12},{1,3},{3,1},... | collective-permute-start | bytes 294920 | tf_op jit(solution)/shard_map/ppermute | solution.py:406
  39.3 4.6 %collective-permute-start.10 = (bf16[96,512]{1,0:T(8,128)(2,1)S(1)}, bf16[96,512]{1,0:T(8,128)(2,1)S(1)}, u32[]{:S(2)}, u32[]{:S(2)}) collective-permute-start(bf16[96,512]{1,0:T(8,128)(2,1)S(1)} %collective-permute-done.6.rest_3_), channel_id=1, source_target_pairs={{0,2},{2,0},{4,6},{6,4},{8,10},{10,8},{12,14},{14,12},{1,3},{3,1},... | collective-permute-start | bytes 294920 | tf_op jit(solution)/shard_map/ppermute | solution.py:406
